TPU v7x, 128 devices: a whole 4x4x4 slice. The times are simulated.
128 devices in a mesh: px: 16 (over z, y), py: 8 (over x, core).
Axes of the slice: x: 4, y: 4, z: 4, core: 2. Of those that a mesh axis runs over, the one named last changes fastest.
Arguments:
- right_side: float32 [4, 5, 5, 5, 32, 16, 128], P(None, None, None, None, 'px', 'py'), may hold values from -6 to 6
- first_guess: float32 [4, 5, 5, 5, 32, 16, 128], P(None, None, None, None, 'px', 'py'), may hold values from -6 to 6
- coefficient: float32 [32, 16, 128], P('px', 'py'), may hold values from 0.2 to 2
- modal_basis: float32 [5, 5], replicated, may hold values from -1 to 1, as said below
- modal_values: float32 [5], replicated, may hold values from 0.5 to 4
- patch_inverse: float32 [256, 256], replicated, may hold values from -0.018 to 0.018
- patch_elements: int32 [65536, 8], P(('px', 'py')), may hold values from 0 to 65535, as said below
- patch_mask: int32 [65536, 8], P(('px', 'py')), may hold values from 0 to 1, as said below
Outputs:
- solution: float32 [4, 5, 5, 5, 32, 16, 128], P(None, None, None, None, 'px', 'py')
Inputs may be any that keep to these rules, and one draw needn't show every extreme that they name: `modal_basis`: an orthogonal matrix. `patch_elements`: element number e = (x 16 + y) * 128 + z. Row r belongs to block b = r // 512 with bx = b // 8 and by = b % 8; every slot of the row, live or padded, names an element with bx * 2 - 1 <= x <= bx * 2 + 2 and by * 2 - 1 <= y <= by * 2 + 2. The live slots of a row name distinct elements that share one mesh vertex. `patch_mask`: padded slots belong to patches of vertices on the boundary of the grid.
All inputs are finite; a program needn't handle non-finite values.
Results may differ from a plain program's by a relative error of at most 0.0001.
Values sent between devices are 32-bit elements; how exact they have to be, the bound alone decides.
A program may use at most 64 MiB of HBM per device.

v0:
```python
import math

import jax
import jax.numpy as jnp
import numpy as np
from jax import lax
from jax.experimental import pallas as pl
from jax.experimental.pallas import tpu as pltpu
from jax.sharding import PartitionSpec as P

MESH = pl.DeviceIdType.MESH
F32 = jnp.float32
BF16 = jnp.bfloat16
DIRS = ((1, 0), (-1, 0), (0, 1), (0, -1), (1, 1), (1, -1), (-1, 1), (-1, -1))
LANES = 512


def linear_values():
    root = np.float32(math.sqrt(3.0 / 7.0))
    points = np.array([-1.0, -root, 0.0, root, 1.0], np.float32)
    half = np.float32(0.5)
    return (1 - points) * half, (1 + points) * half


def column_table():
    table = np.full((8, 640), 7, np.int32)
    table[3] = 9

    def put(column, i, j, k, f=9):
        table[0:4, column] = (i, j, k, f)

    for n in range(125):
        put(n, n // 25, n // 5 % 5, n % 5)
    for g in range(25):
        u, v = g // 5, g % 5
        put(128 + g, 4, u, v)
        put(160 + g, 0, u, v)
        put(192 + u * 8 + v, u, 4, v)
        put(232 + u * 8 + v, u, 0, v)
        put(272 + g, u, v, 4)
        put(304 + g, u, v, 0)
    for r in range(32):
        a, b, f, c = r // 16, r // 8 % 2, r // 2 % 4, r % 2
        for copy in range(3):
            put(384 + 32 * copy + r, 5 + a, 5 + b, 5 + c, f)
        put(512 + 64 + r, 5 + a, 5 + b, 4 if c == 0 else 0, f)
    for r in range(16):
        h, f, c = r // 8, r // 2 % 4, r % 2
        put(512 + r, 4, 5 + h, 5 + c, f)
        put(528 + r, 0, 5 + h, 5 + c, f)
        put(544 + r, 5 + h, 4, 5 + c, f)
        put(560 + r, 5 + h, 0, 5 + c, f)
    return table


def split(value):
    high = value.astype(BF16)
    return high, (value - high.astype(F32)).astype(BF16)


def dot(a, b):
    return lax.dot_general(a, b, (((1,), (0,)), ((), ())), preferred_element_type=F32)


def dot_nt(a, b):
    return lax.dot_general(a, b, (((1,), (1,)), ((), ())), preferred_element_type=F32)


def mm3(ah, al, x):
    xh, xl = split(x)
    return dot(ah, xh) + dot(ah, xl) + dot(al, xh)


def iota(shape, dim):
    return lax.broadcasted_iota(jnp.int32, shape, dim)


def a_half(v, a):
    return v[16 * a : 16 * a + 16]


def b_half(v, b):
    return jnp.concatenate([v[8 * b : 8 * b + 8], v[16 + 8 * b : 24 + 8 * b]], axis=0)


def add_a(v, a, h):
    parts = [v[0:16], v[16:32]]
    parts[a] = parts[a] + h
    return jnp.concatenate(parts, axis=0)


def add_b(v, b, h):
    parts = [v[0:8], v[8:16], v[16:24], v[24:32]]
    parts[b] = parts[b] + h[0:8]
    parts[2 + b] = parts[2 + b] + h[8:16]
    return jnp.concatenate(parts, axis=0)


def rows_to(v, rows):
    return jnp.concatenate([v, jnp.zeros((rows - v.shape[0], v.shape[1]), v.dtype)], axis=0)


def from_next(v):
    lane = iota(v.shape, 1)
    return jnp.where(lane == 127, 0.0, pltpu.roll(v, 127, 1))


def from_previous(v):
    lane = iota(v.shape, 1)
    return jnp.where(lane == 0, 0.0, pltpu.roll(v, 1, 1))


def by_column(fn, v):
    return jnp.concatenate([fn(v[:, 128 * c : 128 * c + 128]) for c in range(4)], axis=1)


def kernel(
    nx, ny,
    xa, xx, xy, xz, ba, coef_h, ub, mv, pinv_h, pe_h, pm_h, tab_h,
    out_h,
    xin, bin_, nfx, nfy, nfz, coef, pinv, pe, pm, tab,
    bt_h, bt_l, bte_h, bte_l, bb_h, bb_l, fb_h, fb_l,
    qc_h, qc_l, qf_h, qf_l, tc, tf_h, tf_l, mi_h, mi_l,
    xhat, bhat, dinv, oh, xs_h, xs_l, ts_h, ts_l,
    cp, gath, wh, wl, ans, ap, vv,
    sx, sy, rx, ry, fz, s2, r2, s3, r3, outv,
    lsem, ssem1, rsem1, ssemf, rsemf, ssem2, rsem2, ssem3, rsem3,
):
    px, py = lax.axis_index("px"), lax.axis_index("py")

    def peer(dx, dy):
        return (lax.rem(px + dx + nx, nx), lax.rem(py + dy + ny, ny))

    local = []

    def load(src, dst):
        copy = pltpu.make_async_copy(src, dst, lsem.at[len(local)])
        copy.start()
        local.append(copy)

    load(tab_h, tab)
    load(coef_h, coef)
    load(xa.at[:, :, 0, :], xin)
    load(ba.at[:, :, 0, :], bin_)
    load(pe_h, pe)
    load(pm_h, pm)
    load(pinv_h, pinv)
    load(xx.at[:, 0, :, 1, 0, :], nfx.at[0, :, :, pl.ds(0, 256)])
    load(xx.at[:, 4, :, 0, 0, :], nfx.at[1, :, :, pl.ds(256, 256)])
    for x in range(2):
        load(xy.at[:, :, 0, :, x, 1, 0, :], nfy.at[0, :, :, :, pl.ds(256 * x, 128)])
        load(xy.at[:, :, 4, :, x, 0, 0, :], nfy.at[1, :, :, :, pl.ds(256 * x + 128, 128)])
    load(xz.at[:, :, 0, 0, :], nfz.at[0])
    load(xz.at[:, :, 4, 0, :], nfz.at[1])

    barrier = pltpu.get_barrier_semaphore()
    for dx, dy in DIRS:
        pl.semaphore_signal(barrier, inc=1, device_id=peer(dx, dy), device_id_type=MESH)
    pl.semaphore_wait(barrier, 8)

    sent = []

    def send(src, dst, ssem, rsem, to):
        copy = pltpu.make_async_remote_copy(
            src_ref=src, dst_ref=dst, send_sem=ssem, recv_sem=rsem, device_id=to, device_id_type=MESH
        )
        copy.start()
        sent.append(copy)
        return copy

    first = [
        send(xx.at[:, 4, :, 1, 0, :], nfx.at[1, :, :, pl.ds(0, 256)], ssem1.at[0], rsem1.at[0], peer(1, 0)),
        send(xx.at[:, 0, :, 0, 0, :], nfx.at[0, :, :, pl.ds(256, 256)], ssem1.at[1], rsem1.at[1], peer(-1, 0)),
    ]
    for x in range(2):
        first.append(
            send(xy.at[:, :, 4, :, x, 1, 0, :], nfy.at[1, :, :, :, pl.ds(256 * x, 128)],
                 ssem1.at[2 + 2 * x], rsem1.at[2 + 2 * x], peer(0, 1))
        )
        first.append(
            send(xy.at[:, :, 0, :, x, 0, 0, :], nfy.at[0, :, :, :, pl.ds(256 * x + 128, 128)],
                 ssem1.at[3 + 2 * x], rsem1.at[3 + 2 * x], peer(0, -1))
        )

    basis = [[ub[p, q] for q in range(5)] for p in range(5)]
    for weights in linear_values():
        basis.append([sum(float(weights[i]) * basis[i][q] for i in range(5)) for q in range(5)])
    spectrum = [mv[q] for q in range(5)]
    local[0].wait()
    local[1].wait()

    def mode_index(shape):
        row = iota(shape, 0)
        i = (row * 41) >> 10
        rest = row - 25 * i
        j = (rest * 13) >> 6
        return i, j, rest - 5 * j

    def block(start):
        modes = mode_index((128, 128))
        result = None
        for d in range(3):
            index = tab[d : d + 1, start : start + 128]
            hits = [index == p for p in range(7)]
            grown = jnp.zeros((128, 128), F32)
            for q in range(5):
                line = jnp.zeros((1, 128), F32)
                for p in range(7):
                    line = jnp.where(hits[p], basis[p][q], line)
                grown = jnp.where(modes[d] == q, line, grown)
            result = grown if result is None else result * grown
        return result

    nodes = block(0)
    bt_h[...], bt_l[...] = split(nodes)
    bb_h[...], bb_l[...] = split(nodes.T)
    for part in range(2):
        faces = block(128 + 128 * part)
        span = pl.ds(128 * part, 128)
        bte_h[:, span], bte_l[:, span] = split(faces)
        fb_h[span, :], fb_l[span, :] = split(faces.T)
    field = tab[3:4, 384:512]
    coarse_block = block(384)
    copy_of = iota((128, 128), 1)
    for f in range(4):
        part = jnp.where(field == f, coarse_block, 0.0)
        high, low = split(part)
        tc[pl.ds(128 * f, 128), :] = jnp.where(copy_of < 64, high.astype(F32), low.astype(F32)).astype(BF16)
        turned = part.T
        qc_h[:, pl.ds(128 * f, 128)], qc_l[:, pl.ds(128 * f, 128)] = split(turned[0:32])
    field = tab[3:4, 512:640]
    face_block = block(512)
    for f in range(4):
        part = jnp.where(field == f, face_block, 0.0)
        tf_h[pl.ds(128 * f, 128), :], tf_l[pl.ds(128 * f, 128), :] = split(part)
        turned = part.T
        qf_h[:, pl.ds(128 * f, 128)], qf_l[:, pl.ds(128 * f, 128)] = split(turned[0:96])

    modes = mode_index((128, 128))
    total = jnp.zeros((128, 128), F32)
    for d in range(3):
        for q in range(5):
            total = jnp.where(modes[d] == q, total + spectrum[q], total)

    def diagonal(c):
        return total * coef[c : c + 1, :] + 1.0

    for c in range(4):
        dinv[:, pl.ds(128 * c, 128)] = 1.0 / diagonal(c)

    local[2].wait()
    local[3].wait()
    for f in range(4):
        xhat[f] = mm3(bt_h[...], bt_l[...], rows_to(xin[f], 128))
        bhat[f] = mm3(bt_h[...], bt_l[...], rows_to(bin_[f], 128))

    local[4].wait()
    local[5].wait()
    elements = pe[...]
    alive = pm[...] != 0
    at_x = (elements >> 11) - 2 * px + 1
    at_y = ((elements >> 7) & 15) - 2 * py + 1
    at_z = elements & 127

    def least(v, most):
        return jnp.minimum(jnp.min(jnp.where(alive, v, most), axis=0, keepdims=True), most)

    low_x, low_y, low_z = least(at_x, 2), least(at_y, 2), least(at_z, 126)
    key = (low_x * 3 + low_y) * 128 + low_z
    place = (at_x - low_x) * 4 + (at_y - low_y) * 2 + (at_z - low_z)
    place = jnp.where(alive, place, 99)
    vertex = iota((128, LANES), 0)
    for v in range(9):
        oh[pl.ds(128 * v, 128), :] = jnp.where(vertex + 128 * v == key, 1.0, 0.0).astype(BF16)

    local[6].wait()
    r = iota((256, 256), 0)
    source = (((r >> 1) & 3) * 8 + ((r >> 4) & 1) * 4 + ((r >> 3) & 1) * 2 + (r & 1)) * 8 + (r >> 5)
    order = jnp.where(iota((256, 256), 1) == source, 1.0, 0.0).astype(BF16)
    for piece, target in zip(split(pinv[...]), (mi_h, mi_l)):
        target[...] = dot_nt(dot(order, piece).astype(BF16), order).astype(BF16)

    has = {
        (1, 0): jnp.where(px < nx - 1, 1.0, 0.0),
        (-1, 0): jnp.where(px > 0, 1.0, 0.0),
        (0, 1): jnp.where(py < ny - 1, 1.0, 0.0),
        (0, -1): jnp.where(py > 0, 1.0, 0.0),
    }
    lane = iota((1, LANES), 1)
    upper_x = jnp.where(lane >= 256, has[(1, 0)], 1.0)
    lower_x = jnp.where(lane < 256, has[(-1, 0)], 1.0)
    upper_y = jnp.where(((lane >> 7) & 1) == 1, has[(0, 1)], 1.0)
    lower_y = jnp.where(((lane >> 7) & 1) == 0, has[(0, -1)], 1.0)

    for copy in local[7:]:
        copy.wait()
    for copy in first:
        copy.wait_recv()

    for f in range(4):
        parts = [
            rows_to(nfx[0, f], 32) * upper_x,
            rows_to(nfx[1, f], 32) * lower_x,
        ]
        parts += [rows_to(nfy[0, f, i], 8) * upper_y for i in range(5)]
        parts += [rows_to(nfy[1, f, i], 8) * lower_y for i in range(5)]
        parts.append(by_column(from_next, rows_to(nfz[0, f], 32)))
        parts.append(by_column(from_previous, rows_to(nfz[1, f], 32)))
        parts.append(jnp.zeros((48, LANES), F32))
        around = mm3(bte_h[...], bte_l[...], jnp.concatenate(parts, axis=0))
        loaded = bhat[f] + 0.5 * around
        x0 = xhat[f]
        x1 = 0.2 * x0 + 0.8 * (dinv[...] * loaded)
        diag = jnp.concatenate([diagonal(c) for c in range(4)], axis=1)
        rest = bhat[f] - 0.2 * (diag * x0) - 0.8 * loaded
        xhat[f] = x1
        rows = pl.ds(128 * f, 128)
        xs_h[rows, :], xs_l[rows, :] = split(x1)
        ts_h[rows, :], ts_l[rows, :] = split(rest)

    inner = dot(qc_h[...], ts_h[...]) + dot(qc_h[...], ts_l[...]) + dot(qc_l[...], ts_h[...])
    rim = 0.5 * (dot(qf_h[...], xs_h[...]) + dot(qf_h[...], xs_l[...]) + dot(qf_l[...], xs_h[...]))
    up_row = ((iota((32, 128), 0) & 1) == 1)

    def rim_of(start, size, c):
        return rim[start : start + size, 128 * c : 128 * c + 128]

    own = {}
    for x in range(2):
        for y in range(2):
            c = 2 * x + y
            v = inner[:, 128 * c : 128 * c + 128]
            faces = rim_of(64, 32, c)
            v = v + jnp.where(up_row, from_next(faces), from_previous(faces))
            v = add_a(v, 0, rim_of(0, 16, y)) if x == 1 else add_a(v, 1, rim_of(16, 16, 2 + y))
            v = add_b(v, 0, rim_of(32, 16, 2 * x)) if y == 1 else add_b(v, 1, rim_of(48, 16, 2 * x + 1))
            own[(x, y)] = v
    hx = {(1, y): rim_of(0, 16, 2 + y) for y in range(2)} | {(-1, y): rim_of(16, 16, y) for y in range(2)}
    hy = {(1, x): rim_of(32, 16, 2 * x + 1) for x in range(2)} | {(-1, x): rim_of(48, 16, 2 * x) for x in range(2)}

    def edge(d):
        return 1 if d == 1 else 0

    def exchange(blocks, sbuf, rbuf, ssem, rsem):
        copies = []
        for n, (dx, dy) in enumerate(DIRS):
            at = 0
            for v in blocks(dx, dy):
                sbuf[n, pl.ds(at, v.shape[0]), :] = v
                at += v.shape[0]
            copies.append(
                send(sbuf.at[n, pl.ds(0, at)], rbuf.at[n, pl.ds(0, at)], ssem.at[n], rsem.at[n], peer(dx, dy))
            )
        return copies

    def residual_blocks(dx, dy):
        x, y = edge(dx), edge(dy)
        if dy == 0:
            return [own[(x, 0)], own[(x, 1)], hx[(dx, 0)], hx[(dx, 1)], hy[(1, x)], hy[(-1, x)]]
        if dx == 0:
            return [own[(0, y)], own[(1, y)], hy[(dy, 0)], hy[(dy, 1)], hx[(1, y)], hx[(-1, y)]]
        return [own[(x, y)], hx[(dx, y)], hy[(dy, x)]]

    second = exchange(residual_blocks, s2, r2, ssem2, rsem2)

    for f in range(4):
        rows = pl.ds(128 * f, 128)
        for part in range(2):
            span = pl.ds(128 * part, 128)
            faces = (
                dot(fb_h[span, :], xs_h[rows, :])
                + dot(fb_h[span, :], xs_l[rows, :])
                + dot(fb_l[span, :], xs_h[rows, :])
            )
            fz[f, span, :] = faces
        sx[0, f] = fz[f, 0:32, 256:512]
        sx[1, f] = fz[f, 32:64, 0:256]
        for x in range(2):
            sy[0, f, :, pl.ds(128 * x, 128)] = fz[f, 64:104, 256 * x + 128 : 256 * x + 256]
            sy[1, f, :, pl.ds(128 * x, 128)] = fz[f, 104:144, 256 * x : 256 * x + 128]
    whole = [
        send(sx.at[0], rx.at[0], ssemf.at[0], rsemf.at[0], peer(1, 0)),
        send(sx.at[1], rx.at[1], ssemf.at[1], rsemf.at[1], peer(-1, 0)),
        send(sy.at[0], ry.at[0], ssemf.at[2], rsemf.at[2], peer(0, 1)),
        send(sy.at[1], ry.at[1], ssemf.at[3], rsemf.at[3], peer(0, -1)),
    ]

    def sender_is_there(dx, dy):
        there = 1.0
        if dx:
            there = there * has[(-dx, 0)]
        if dy:
            there = there * has[(0, -dy)]
        return there

    for copy in second:
        copy.wait_recv()
    field_of = {}

    def put(at, v):
        field_of[at] = field_of[at] + v if at in field_of else v

    for at, v in own.items():
        put(at, v)
    late = []
    for y in range(2):
        late += [("a", 0, (2, y), hx[(1, y)]), ("a", 1, (-1, y), hx[(-1, y)])]
        late += [("b", 0, (y, 2), hy[(1, y)]), ("b", 1, (y, -1), hy[(-1, y)])]
    for n, (dx, dy) in enumerate(DIRS):
        x, y = edge(dx), edge(dy)
        there = sender_is_there(dx, dy)
        side_a, side_b = (0 if dx == 1 else 1), (0 if dy == 1 else 1)
        if dy == 0:
            for t in range(2):
                put((x - 2 * dx, t), r2[n, 32 * t : 32 * t + 32, :])
                late.append(("a", side_a, (x - dx, t), r2[n, 64 + 16 * t : 80 + 16 * t, :] * there))
            late.append(("b", 0, (x - 2 * dx, 2), r2[n, 96:112, :] * there))
            late.append(("b", 1, (x - 2 * dx, -1), r2[n, 112:128, :] * there))
        elif dx == 0:
            for t in range(2):
                put((t, y - 2 * dy), r2[n, 32 * t : 32 * t + 32, :])
                late.append(("b", side_b, (t, y - dy), r2[n, 64 + 16 * t : 80 + 16 * t, :] * there))
            late.append(("a", 0, (2, y - 2 * dy), r2[n, 96:112, :] * there))
            late.append(("a", 1, (-1, y - 2 * dy), r2[n, 112:128, :] * there))
        else:
            put((x - 2 * dx, y - 2 * dy), r2[n, 0:32, :])
            late.append(("a", side_a, (x - dx, y - 2 * dy), r2[n, 32:48, :] * there))
            late.append(("b", side_b, (x - 2 * dx, y - dy), r2[n, 48:64, :] * there))
    for kind, side, at, v in late:
        field_of[at] = add_a(field_of[at], side, v) if kind == "a" else add_b(field_of[at], side, v)

    for (x, y), v in field_of.items():
        moved = pltpu.roll(v, 127, 1)
        for z, value in enumerate((v, moved)):
            pieces = split(value)
            for sx_, sy_ in ((0, 0), (0, 1), (1, 0), (1, 1)):
                vx, vy = x + 1 - sx_, y + 1 - sy_
                if 0 <= vx <= 2 and 0 <= vy <= 2:
                    p = sx_ * 4 + sy_ * 2 + z
                    for t in range(2):
                        cp[pl.ds(256 * t + 32 * p, 32), pl.ds(128 * (3 * vx + vy), 128)] = pieces[t]
    gath[...] = dot(cp[pl.ds(0, 256), :], oh[...]) + dot(cp[pl.ds(256, 256), :], oh[...])
    for s in range(8):
        slot = jnp.broadcast_to(place[s : s + 1, :], (32, LANES))
        value = jnp.zeros((32, LANES), F32)
        for p in range(8):
            value = jnp.where(slot == p, gath[pl.ds(32 * p, 32), :], value)
        rows = pl.ds(32 * s, 32)
        wh[rows, :], wl[rows, :] = split(value)
    ans[...] = dot(mi_h[...], wh[...]) + dot(mi_h[...], wl[...]) + dot(mi_l[...], wh[...])
    for p in range(8):
        value = jnp.zeros((32, LANES), F32)
        for s in range(8):
            slot = jnp.broadcast_to(place[s : s + 1, :], (32, LANES))
            value = jnp.where(slot == p, ans[pl.ds(32 * s, 32), :], value)
        ap[pl.ds(32 * p, 32), :], ap[pl.ds(256 + 32 * p, 32), :] = split(value)
    vv[...] = dot_nt(ap[pl.ds(0, 256), :], oh[...]) + dot_nt(ap[pl.ds(256, 256), :], oh[...])
    spread = {}
    for x in range(-1, 3):
        for y in range(-1, 3):
            sums = [None, None]
            for sx_, sy_ in ((0, 0), (0, 1), (1, 0), (1, 1)):
                vx, vy = x + 1 - sx_, y + 1 - sy_
                if 0 <= vx <= 2 and 0 <= vy <= 2:
                    for z in range(2):
                        p = sx_ * 4 + sy_ * 2 + z
                        v = vv[pl.ds(32 * p, 32), pl.ds(128 * (3 * vx + vy), 128)]
                        sums[z] = v if sums[z] is None else sums[z] + v
            spread[(x, y)] = sums[0] + pltpu.roll(sums[1], 1, 1)

    def correction_blocks(dx, dy):
        x, y = edge(dx), edge(dy)
        if dy == 0:
            return [
                spread[(x + dx, 0)], spread[(x + dx, 1)], a_half(spread[(x, 0)], x), a_half(spread[(x, 1)], x),
                b_half(spread[(x + dx, 2)], 0), b_half(spread[(x + dx, -1)], 1),
            ]
        if dx == 0:
            return [
                spread[(0, y + dy)], spread[(1, y + dy)], b_half(spread[(0, y)], y), b_half(spread[(1, y)], y),
                a_half(spread[(2, y + dy)], 0), a_half(spread[(-1, y + dy)], 1),
            ]
        return [spread[(x + dx, y + dy)], a_half(spread[(x, y + dy)], x), b_half(spread[(x + dx, y)], y)]

    third = exchange(correction_blocks, s3, r3, ssem3, rsem3)

    for copy in whole:
        copy.wait_recv()
    for f in range(4):
        x_up = jnp.concatenate([fz[f, 32:64, 256:512], rx[1, f]], axis=1) * upper_x
        x_down = jnp.concatenate([rx[0, f], fz[f, 0:32, 0:256]], axis=1) * lower_x
        y_up, y_down = [], []
        for x in range(2):
            y_up += [fz[f, 104:144, 256 * x + 128 : 256 * x + 256], ry[1, f, :, 128 * x : 128 * x + 128]]
            y_down += [ry[0, f, :, 128 * x : 128 * x + 128], fz[f, 64:104, 256 * x : 256 * x + 128]]
        parts = [
            x_up, x_down,
            jnp.concatenate(y_up, axis=1) * upper_y,
            jnp.concatenate(y_down, axis=1) * lower_y,
            by_column(from_next, fz[f, 176:208, :]),
            by_column(from_previous, fz[f, 144:176, :]),
            jnp.zeros((48, LANES), F32),
        ]
        around = mm3(bte_h[...], bte_l[...], jnp.concatenate(parts, axis=0))
        xhat[f] = 0.2 * xhat[f] + 0.8 * (dinv[...] * (bhat[f] + 0.5 * around))

    for copy in third:
        copy.wait_recv()
    fixed = {at: spread[at] for at in own}
    near_x = {(2, y): a_half(spread[(2, y)], 0) for y in range(2)} | {
        (-1, y): a_half(spread[(-1, y)], 1) for y in range(2)
    }
    near_y = {(x, 2): b_half(spread[(x, 2)], 0) for x in range(2)} | {
        (x, -1): b_half(spread[(x, -1)], 1) for x in range(2)
    }
    for n, (dx, dy) in enumerate(DIRS):
        x, y = edge(dx), edge(dy)
        if dy == 0:
            for t in range(2):
                fixed[(x - dx, t)] += r3[n, 32 * t : 32 * t + 32, :]
                near_x[(x - 2 * dx, t)] += r3[n, 64 + 16 * t : 80 + 16 * t, :]
            near_y[(x - dx, 2)] += r3[n, 96:112, :]
            near_y[(x - dx, -1)] += r3[n, 112:128, :]
        elif dx == 0:
            for t in range(2):
                fixed[(t, y - dy)] += r3[n, 32 * t : 32 * t + 32, :]
                near_y[(t, y - 2 * dy)] += r3[n, 64 + 16 * t : 80 + 16 * t, :]
            near_x[(2, y - dy)] += r3[n, 96:112, :]
            near_x[(-1, y - dy)] += r3[n, 112:128, :]
        else:
            fixed[(x - dx, y - dy)] += r3[n, 0:32, :]
            near_x[(x - 2 * dx, y - dy)] += r3[n, 32:48, :]
            near_y[(x - dx, y - 2 * dy)] += r3[n, 48:64, :]

    columns, rims = [], []
    for x in range(2):
        for y in range(2):
            v = fixed[(x, y)]
            columns.append(v)
            rims.append(
                jnp.concatenate(
                    [
                        a_half(fixed[(1, y)], 0) if x == 0 else near_x[(2, y)] * has[(1, 0)],
                        a_half(fixed[(0, y)], 1) if x == 1 else near_x[(-1, y)] * has[(-1, 0)],
                        b_half(fixed[(x, 1)], 0) if y == 0 else near_y[(x, 2)] * has[(0, 1)],
                        b_half(fixed[(x, 0)], 1) if y == 1 else near_y[(x, -1)] * has[(0, -1)],
                        jnp.where(up_row, from_previous(v), from_next(v)),
                        jnp.zeros((32, 128), F32),
                    ],
                    axis=0,
                )
            )
    ch, cl = split(jnp.concatenate(columns, axis=1))
    stacked = jnp.concatenate([ch, cl, ch, jnp.zeros((32, LANES), BF16)], axis=0)
    rh, rl = split(jnp.concatenate(rims, axis=1))
    for f in range(4):
        rows = pl.ds(128 * f, 128)
        direct = dot(tc[rows, :], stacked)
        coupled = dot(tf_h[rows, :], rh) + dot(tf_h[rows, :], rl) + dot(tf_l[rows, :], rh)
        final = xhat[f] + 0.2 * direct + 0.4 * (dinv[...] * coupled)
        outv[f] = mm3(bb_h[...], bb_l[...], final)[0:125]
    done = pltpu.make_async_copy(outv, out_h.at[:, :, 0, :], lsem.at[len(local)])
    done.start()
    for copy in sent:
        copy.wait_send()
    done.wait()


def solution(mesh):
    nx, ny = mesh.shape["px"], mesh.shape["py"]
    table = column_table()

    def per_device(
        right_side, first_guess, coefficient, modal_basis, modal_values, patch_inverse, patch_elements, patch_mask
    ):
        any_ = pl.BlockSpec(memory_space=pl.ANY)
        smem = pl.BlockSpec(memory_space=pltpu.SMEM)

        def body(*refs):
            kernel(nx, ny, *refs)

        def f32(*shape):
            return pltpu.VMEM(shape, F32)

        def b16(*shape):
            return pltpu.VMEM(shape, BF16)

        dma = pltpu.SemaphoreType.DMA
        out = pl.pallas_call(
            body,
            out_shape=jax.ShapeDtypeStruct((4, 125, 1, 512), F32),
            in_specs=[any_] * 6 + [smem] * 2 + [any_] * 4,
            out_specs=any_,
            scratch_shapes=[
                f32(4, 125, 512), f32(4, 125, 512), f32(2, 4, 25, 512), f32(2, 4, 5, 5, 512), f32(2, 4, 25, 512),
                f32(4, 128), f32(256, 256), pltpu.VMEM((8, 512), jnp.int32), pltpu.VMEM((8, 512), jnp.int32),
                pltpu.VMEM((8, 640), jnp.int32),
                b16(128, 128), b16(128, 128), b16(128, 256), b16(128, 256), b16(128, 128), b16(128, 128),
                b16(256, 128), b16(256, 128),
                b16(32, 512), b16(32, 512), b16(96, 512), b16(96, 512),
                b16(512, 128), b16(512, 128), b16(512, 128), b16(256, 256), b16(256, 256),
                f32(4, 128, 512), f32(4, 128, 512), f32(128, 512), b16(1152, 512),
                b16(512, 512), b16(512, 512), b16(512, 512), b16(512, 512),
                b16(512, 1152), f32(256, 512), b16(256, 512), b16(256, 512), f32(256, 512), b16(512, 512),
                f32(256, 1152),
                f32(2, 4, 32, 256), f32(2, 4, 40, 256), f32(2, 4, 32, 256), f32(2, 4, 40, 256), f32(4, 256, 512),
                f32(8, 128, 128), f32(8, 128, 128), f32(8, 128, 128), f32(8, 128, 128), f32(4, 125, 512),
                dma((16,)), dma((6,)), dma((6,)), dma((4,)), dma((4,)), dma((8,)), dma((8,)), dma((8,)), dma((8,)),
            ],
            compiler_params=pltpu.CompilerParams(
                collective_id=0, has_side_effects=True, vmem_limit_bytes=48 * 1024 * 1024
            ),
        )(
            first_guess.reshape(4, 125, 1, 512),
            first_guess.reshape(4, 5, 25, 2, 1, 256),
            first_guess.reshape(4, 5, 5, 5, 2, 2, 1, 128),
            first_guess.reshape(4, 25, 5, 1, 512),
            right_side.reshape(4, 125, 1, 512),
            coefficient.reshape(4, 128),
            modal_basis,
            modal_values,
            patch_inverse,
            patch_elements.T,
            patch_mask.T,
            jnp.asarray(table),
        )
        return out.reshape(4, 5, 5, 5, 2, 2, 128)

    grid = P(None, None, None, None, "px", "py", None)
    rows = P(("px", "py"), None)
    return jax.shard_map(
        per_device,
        mesh=mesh,
        in_specs=(grid, grid, P("px", "py", None), P(), P(), P(), rows, rows),
        out_specs=grid,
        check_vma=False,
    )
```

profile of v0, /device:TPU:1, one launch (start us, length us, event | category | flops | bytes accessed | tf_op | source)
XLA Modules:
  0.0 42.5 jit_solution(17318208923759372264)
XLA Ops:
  0.0 0.0 copy-start.6
  0.0 0.0 copy-start.7
  0.0 0.0 copy-start.8
  0.0 0.7 %copy-done.6 = f32[5,5]{1,0:T(8,128)S(1)} copy-done((f32[5,5]{1,0:T(8,128)S(1)}, f32[5,5]{1,0:T(8,128)}, u32[]{:S(2)}) %copy-start.6) | copy-done | bytes 124
  0.7 0.0 copy-done.7
  0.7 0.0 copy-done.8
  0.7 0.0 copy-start
  0.7 1.2 %copy-done = f32[4,5,5,5,2,2,128]{6,5,4,3,2,1,0:T(2,128)S(1)} copy-done((f32[4,5,5,5,2,2,128]{6,5,4,3,2,1,0:T(2,128)S(1)}, f32[4,5,5,5,2,2,128]{6,5,4,3,2,1,0:T(2,128)}, u32[]{:S(2)}) %copy-start) | copy-done | bytes 1024024
  1.9 0.0 copy-start.1
  1.9 1.2 %copy-done.1 = f32[4,5,5,5,2,2,128]{6,5,4,3,2,1,0:T(2,128)S(1)} copy-done((f32[4,5,5,5,2,2,128]{6,5,4,3,2,1,0:T(2,128)S(1)}, f32[4,5,5,5,2,2,128]{6,5,4,3,2,1,0:T(2,128)}, u32[]{:S(2)}) %copy-start.1) | copy-done | bytes 1024024
  3.1 0.0 copy-start.2
  3.1 0.9 %copy-done.2 = f32[256,256]{1,0:T(8,128)S(1)} copy-done((f32[256,256]{1,0:T(8,128)S(1)}, f32[256,256]{1,0:T(8,128)}, u32[]{:S(2)}) %copy-start.2) | copy-done | bytes 262168
  4.1 0.0 copy-start.3
  4.1 0.7 %copy-done.3 = s32[8,640]{1,0:T(8,128)S(1)} copy-done((s32[8,640]{1,0:T(8,128)S(1)}, s32[8,640]{1,0:T(8,128)}, u32[]{:S(2)}) %copy-start.3) | copy-done | bytes 20504
  4.8 0.0 copy-start.4
  4.8 0.7 %copy-done.4 = s32[512,8]{0,1:T(8,128)S(1)} copy-done((s32[512,8]{0,1:T(8,128)S(1)}, s32[512,8]{0,1:T(8,128)}, u32[]{:S(2)}) %copy-start.4) | copy-done | bytes 16408
  5.5 0.0 copy-start.5
  5.5 0.7 %copy-done.5 = s32[512,8]{0,1:T(8,128)S(1)} copy-done((s32[512,8]{0,1:T(8,128)S(1)}, s32[512,8]{0,1:T(8,128)}, u32[]{:S(2)}) %copy-start.5) | copy-done | bytes 16408
  6.2 35.2 %shard_map.91 = f32[4,125,1,512]{3,2,1,0:T(1,128)S(1)} custom-call(f32[4,125,1,512]{3,2,1,0:T(1,128)S(1)} %bitcast.9, f32[4,5,25,2,1,256]{5,4,3,2,1,0:T(1,128)S(1)} %bitcast.10, f32[4,5,5,5,2,2,1,128]{7,6,5,4,3,2,1,0:T(1,128)S(1)} %bitcast.11, f32[4,25,5,1,512]{4,3,2,1,0:T(1,128)S(1)} %bitcast.12, f32[4,125,1,512]{3,2,1,0:T(1,128)S(1)} %bitcast.14, ...), custom_call_target="tpu_custom_call" | custom-call | tf_op jit(solution)/shard_map/pallas_call | solution.py:589
  41.5 1.0 %copy.11 = f32[4,5,5,5,2,2,128]{6,5,4,3,2,1,0:T(2,128)} copy(f32[4,5,5,5,2,2,128]{6,5,4,3,2,1,0:T(2,128)S(1)} %bitcast.13) | data formatting | bytes 2048000
Async XLA Ops:
  0.0 0.7 %copy-start.6 = (f32[5,5]{1,0:T(8,128)S(1)}, f32[5,5]{1,0:T(8,128)}, u32[]{:S(2)}) copy-start(f32[5,5]{1,0:T(8,128)} %refs_6_.1) | copy-start | bytes 304
  0.0 0.7 %copy-start.7 = (f32[2,2,128]{2,1,0:T(2,128)S(1)}, f32[2,2,128]{2,1,0:T(2,128)}, u32[]{:S(2)}) copy-start(f32[2,2,128]{2,1,0:T(2,128)} %param.11) | copy-start | bytes 6148
  0.0 0.7 %copy-start.8 = (f32[5]{0:T(128)S(1)}, f32[5]{0:T(128)}, u32[]{:S(2)}) copy-start(f32[5]{0:T(128)} %refs_7_.1) | copy-start | bytes 64
  0.7 1.2 %copy-start = (f32[4,5,5,5,2,2,128]{6,5,4,3,2,1,0:T(2,128)S(1)}, f32[4,5,5,5,2,2,128]{6,5,4,3,2,1,0:T(2,128)}, u32[]{:S(2)}) copy-start(f32[4,5,5,5,2,2,128]{6,5,4,3,2,1,0:T(2,128)} %param.10) | copy-start | bytes 3072004
  1.9 1.2 %copy-start.1 = (f32[4,5,5,5,2,2,128]{6,5,4,3,2,1,0:T(2,128)S(1)}, f32[4,5,5,5,2,2,128]{6,5,4,3,2,1,0:T(2,128)}, u32[]{:S(2)}) copy-start(f32[4,5,5,5,2,2,128]{6,5,4,3,2,1,0:T(2,128)} %param.9) | copy-start | bytes 3072004
  3.1 0.9 %copy-start.2 = (f32[256,256]{1,0:T(8,128)S(1)}, f32[256,256]{1,0:T(8,128)}, u32[]{:S(2)}) copy-start(f32[256,256]{1,0:T(8,128)} %refs_8_.1) | copy-start | bytes 786436
  4.1 0.7 %copy-start.3 = (s32[8,640]{1,0:T(8,128)S(1)}, s32[8,640]{1,0:T(8,128)}, u32[]{:S(2)}) copy-start(s32[8,640]{1,0:T(8,128)} %constant.2.clone.refs_11_) | copy-start | bytes 61444
  4.8 0.7 %copy-start.4 = (s32[512,8]{0,1:T(8,128)S(1)}, s32[512,8]{0,1:T(8,128)}, u32[]{:S(2)}) copy-start(s32[512,8]{0,1:T(8,128)} %param.15) | copy-start | bytes 49156
  5.5 0.7 %copy-start.5 = (s32[512,8]{0,1:T(8,128)S(1)}, s32[512,8]{0,1:T(8,128)}, u32[]{:S(2)}) copy-start(s32[512,8]{0,1:T(8,128)} %param.16) | copy-start | bytes 49156
where the time goes:
time: 42.9 us; the launch traced here: 42.5 us
  Pallas kernels  35.2 us (82%)
  local copies, waits for them, and re-layouts  7.2 us (17%)
    pallas_call x1, Pallas kernels, per_device(): pl.pallas_call(body, out_shape=jax.ShapeDtypeStruct((4, 125, 1, 512), F32...  35.2 us
    unnamed x19, local copies, waits for them, and re-layouts  7.2 us

commit v1 on v0

--- a/solution.py
+++ b/solution.py
@@ -116,14 +116,14 @@
 
 def kernel(
     nx, ny,
-    xa, xx, xy, xz, ba, coef_h, ub, mv, pinv_h, pe_h, pm_h, tab_h,
-    out_h,
-    xin, bin_, nfx, nfy, nfz, coef, pinv, pe, pm, tab,
+    xa, xx, xy, xz, ba, coef_h, ub_h, mv_h, pinv_h, pe_h, pm_h, tab_h,
+    outv,
+    ub, mv, xin, bin_, nfx, nfy, nfz, coef, pinv, pe, pm, tab,
     bt_h, bt_l, bte_h, bte_l, bb_h, bb_l, fb_h, fb_l,
     qc_h, qc_l, qf_h, qf_l, tc, tf_h, tf_l, mi_h, mi_l,
     xhat, bhat, dinv, oh, xs_h, xs_l, ts_h, ts_l,
     cp, gath, wh, wl, ans, ap, vv,
-    sx, sy, rx, ry, fz, s2, r2, s3, r3, outv,
+    sx, sy, rx, ry, fz, s2, r2, s3, r3,
     lsem, ssem1, rsem1, ssemf, rsemf, ssem2, rsem2, ssem3, rsem3,
 ):
     px, py = lax.axis_index("px"), lax.axis_index("py")
@@ -140,6 +140,8 @@
 
     load(tab_h, tab)
     load(coef_h, coef)
+    load(ub_h, ub)
+    load(mv_h, mv)
     load(xa.at[:, :, 0, :], xin)
     load(ba.at[:, :, 0, :], bin_)
     load(pe_h, pe)
@@ -182,12 +184,12 @@
                  ssem1.at[3 + 2 * x], rsem1.at[3 + 2 * x], peer(0, -1))
         )
 
+    for copy in local[0:4]:
+        copy.wait()
     basis = [[ub[p, q] for q in range(5)] for p in range(5)]
     for weights in linear_values():
         basis.append([sum(float(weights[i]) * basis[i][q] for i in range(5)) for q in range(5)])
     spectrum = [mv[q] for q in range(5)]
-    local[0].wait()
-    local[1].wait()
 
     def mode_index(shape):
         row = iota(shape, 0)
@@ -248,14 +250,14 @@
     for c in range(4):
         dinv[:, pl.ds(128 * c, 128)] = 1.0 / diagonal(c)
 
-    local[2].wait()
-    local[3].wait()
+    local[4].wait()
+    local[5].wait()
     for f in range(4):
         xhat[f] = mm3(bt_h[...], bt_l[...], rows_to(xin[f], 128))
         bhat[f] = mm3(bt_h[...], bt_l[...], rows_to(bin_[f], 128))
 
-    local[4].wait()
-    local[5].wait()
+    local[6].wait()
+    local[7].wait()
     elements = pe[...]
     alive = pm[...] != 0
     at_x = (elements >> 11) - 2 * px + 1
@@ -273,7 +275,7 @@
     for v in range(9):
         oh[pl.ds(128 * v, 128), :] = jnp.where(vertex + 128 * v == key, 1.0, 0.0).astype(BF16)
 
-    local[6].wait()
+    local[8].wait()
     r = iota((256, 256), 0)
     source = (((r >> 1) & 3) * 8 + ((r >> 4) & 1) * 4 + ((r >> 3) & 1) * 2 + (r & 1)) * 8 + (r >> 5)
     order = jnp.where(iota((256, 256), 1) == source, 1.0, 0.0).astype(BF16)
@@ -292,7 +294,7 @@
     upper_y = jnp.where(((lane >> 7) & 1) == 1, has[(0, 1)], 1.0)
     lower_y = jnp.where(((lane >> 7) & 1) == 0, has[(0, -1)], 1.0)
 
-    for copy in local[7:]:
+    for copy in local[9:]:
         copy.wait()
     for copy in first:
         copy.wait_recv()
@@ -558,12 +560,11 @@
         direct = dot(tc[rows, :], stacked)
         coupled = dot(tf_h[rows, :], rh) + dot(tf_h[rows, :], rl) + dot(tf_l[rows, :], rh)
         final = xhat[f] + 0.2 * direct + 0.4 * (dinv[...] * coupled)
-        outv[f] = mm3(bb_h[...], bb_l[...], final)[0:125]
-    done = pltpu.make_async_copy(outv, out_h.at[:, :, 0, :], lsem.at[len(local)])
-    done.start()
+        value = mm3(bb_h[...], bb_l[...], final)
+        for c in range(4):
+            outv[pl.ds(500 * f + c, 125, stride=4), :] = value[0:125, 128 * c : 128 * c + 128]
     for copy in sent:
         copy.wait_send()
-    done.wait()
 
 
 def solution(mesh):
@@ -573,8 +574,7 @@
     def per_device(
         right_side, first_guess, coefficient, modal_basis, modal_values, patch_inverse, patch_elements, patch_mask
     ):
-        any_ = pl.BlockSpec(memory_space=pl.ANY)
-        smem = pl.BlockSpec(memory_space=pltpu.SMEM)
+        hbm = pl.BlockSpec(memory_space=pltpu.HBM)
 
         def body(*refs):
             kernel(nx, ny, *refs)
@@ -584,14 +584,18 @@
 
         def b16(*shape):
             return pltpu.VMEM(shape, BF16)
+
+        def in_hbm(array):
+            return pltpu.with_memory_space_constraint(array, pltpu.HBM)
 
         dma = pltpu.SemaphoreType.DMA
         out = pl.pallas_call(
             body,
-            out_shape=jax.ShapeDtypeStruct((4, 125, 1, 512), F32),
-            in_specs=[any_] * 6 + [smem] * 2 + [any_] * 4,
-            out_specs=any_,
+            out_shape=pltpu.VMEM((2000, 128), F32),
+            in_specs=[hbm] * 12,
+            out_specs=pl.BlockSpec(memory_space=pltpu.VMEM),
             scratch_shapes=[
+                pltpu.SMEM((5, 5), F32), pltpu.SMEM((5,), F32),
                 f32(4, 125, 512), f32(4, 125, 512), f32(2, 4, 25, 512), f32(2, 4, 5, 5, 512), f32(2, 4, 25, 512),
                 f32(4, 128), f32(256, 256), pltpu.VMEM((8, 512), jnp.int32), pltpu.VMEM((8, 512), jnp.int32),
                 pltpu.VMEM((8, 640), jnp.int32),
@@ -604,25 +608,25 @@
                 b16(512, 1152), f32(256, 512), b16(256, 512), b16(256, 512), f32(256, 512), b16(512, 512),
                 f32(256, 1152),
                 f32(2, 4, 32, 256), f32(2, 4, 40, 256), f32(2, 4, 32, 256), f32(2, 4, 40, 256), f32(4, 256, 512),
-                f32(8, 128, 128), f32(8, 128, 128), f32(8, 128, 128), f32(8, 128, 128), f32(4, 125, 512),
-                dma((16,)), dma((6,)), dma((6,)), dma((4,)), dma((4,)), dma((8,)), dma((8,)), dma((8,)), dma((8,)),
+                f32(8, 128, 128), f32(8, 128, 128), f32(8, 128, 128), f32(8, 128, 128),
+                dma((20,)), dma((6,)), dma((6,)), dma((4,)), dma((4,)), dma((8,)), dma((8,)), dma((8,)), dma((8,)),
             ],
             compiler_params=pltpu.CompilerParams(
-                collective_id=0, has_side_effects=True, vmem_limit_bytes=48 * 1024 * 1024
+                collective_id=0, has_side_effects=True, vmem_limit_bytes=60 * 1024 * 1024
             ),
         )(
-            first_guess.reshape(4, 125, 1, 512),
-            first_guess.reshape(4, 5, 25, 2, 1, 256),
-            first_guess.reshape(4, 5, 5, 5, 2, 2, 1, 128),
-            first_guess.reshape(4, 25, 5, 1, 512),
-            right_side.reshape(4, 125, 1, 512),
-            coefficient.reshape(4, 128),
-            modal_basis,
-            modal_values,
-            patch_inverse,
-            patch_elements.T,
-            patch_mask.T,
-            jnp.asarray(table),
+            in_hbm(first_guess.reshape(4, 125, 1, 512)),
+            in_hbm(first_guess.reshape(4, 5, 25, 2, 1, 256)),
+            in_hbm(first_guess.reshape(4, 5, 5, 5, 2, 2, 1, 128)),
+            in_hbm(first_guess.reshape(4, 25, 5, 1, 512)),
+            in_hbm(right_side.reshape(4, 125, 1, 512)),
+            in_hbm(coefficient.reshape(4, 128)),
+            in_hbm(modal_basis),
+            in_hbm(modal_values),
+            in_hbm(patch_inverse),
+            in_hbm(patch_elements.T),
+            in_hbm(patch_mask.T),
+            in_hbm(jnp.asarray(table)),
         )
         return out.reshape(4, 5, 5, 5, 2, 2, 128)
 

time: 42.9 us -> 33.6 us (0.78)
  local copies, waits for them, and re-layouts: 7.2 us -> 0.96 us
  Pallas kernels: 35.2 us -> 32.5 us
    unnamed x19 -> x1, local copies, waits for them, and re-layouts: 7.2 us -> 0.96 us
    pallas_call x1, Pallas kernels: 35.2 us -> 32.5 us  [per_device(): pl.pallas_call(body, out_shape=pltpu.VMEM((2000, 128), F32), in_specs=[hb...]
where the time goes in v1:
time: 33.6 us; the launch traced here: 33.5 us
  Pallas kernels  32.5 us (97%)
  local copies, waits for them, and re-layouts  0.96 us (3%)
    pallas_call x1, Pallas kernels, per_device(): pl.pallas_call(body, out_shape=pltpu.VMEM((2000, 128), F32), in_specs=[hb...  32.5 us
    unnamed x1, local copies, waits for them, and re-layouts  0.96 us

profile of v1, /device:TPU:1, one launch (start us, length us, event | category | flops | bytes accessed | tf_op | source)
XLA Modules:
  0.0 33.5 jit_solution(13400619531332543221)
XLA Ops:
  0.0 32.5 %shard_map.91 = f32[2000,128]{1,0:T(8,128)S(1)} custom-call(f32[4,125,1,512]{3,2,1,0:T(1,128)} %bitcast.10, f32[4,5,25,2,1,256]{5,4,3,2,1,0:T(1,128)} %bitcast.11, f32[4,5,5,5,2,2,1,128]{7,6,5,4,3,2,1,0:T(1,128)} %bitcast.12, f32[4,25,5,1,512]{4,3,2,1,0:T(1,128)} %bitcast.13, f32[4,125,1,512]{3,2,1,0:T(1,128)} %bitcast.14, f32[4,128]{1,0:T(4,128)} %bitcast.17, ...), custom_call_target="tpu_custom_call" | custom-call | tf_op jit(solution)/shard_map/pallas_call | solution.py:592
  32.5 1.0 %copy.11 = f32[4,5,5,5,2,2,128]{6,5,4,3,2,1,0:T(2,128)} copy(f32[4,5,5,5,2,2,128]{6,5,4,3,2,1,0:T(2,128)S(1)} %bitcast.9) | data formatting | bytes 2048000

commit v2 on v1

--- a/solution.py
+++ b/solution.py
@@ -131,6 +131,16 @@
     def peer(dx, dy):
         return (lax.rem(px + dx + nx, nx), lax.rem(py + dy + ny, ny))
 
+    inside = {(1, 0): px < nx - 1, (-1, 0): px > 0, (0, 1): py < ny - 1, (0, -1): py > 0}
+
+    def exists(dx, dy):
+        if dx == 0 or dy == 0:
+            return inside[(dx, dy)]
+        return inside[(dx, 0)] & inside[(0, dy)]
+
+    def unless(condition):
+        return pl.when(jnp.logical_not(condition))
+
     local = []
 
     def load(src, dst):
@@ -156,32 +166,78 @@
     load(xz.at[:, :, 4, 0, :], nfz.at[1])
 
     barrier = pltpu.get_barrier_semaphore()
+    greeted = 0
     for dx, dy in DIRS:
-        pl.semaphore_signal(barrier, inc=1, device_id=peer(dx, dy), device_id_type=MESH)
-    pl.semaphore_wait(barrier, 8)
+        greeted = greeted + jnp.where(exists(dx, dy), 1, 0)
+
+        @pl.when(exists(dx, dy))
+        def _():
+            pl.semaphore_signal(barrier, inc=1, device_id=peer(dx, dy), device_id_type=MESH)
+
+    @unless(inside[(1, 0)])
+    def _():
+        nfx[0, :, :, 256:512] = jnp.zeros((4, 25, 256), F32)
+        rx[1] = jnp.zeros((4, 32, 256), F32)
+
+    @unless(inside[(-1, 0)])
+    def _():
+        nfx[1, :, :, 0:256] = jnp.zeros((4, 25, 256), F32)
+        rx[0] = jnp.zeros((4, 32, 256), F32)
+
+    @unless(inside[(0, 1)])
+    def _():
+        for x in range(2):
+            nfy[0, :, :, :, 256 * x + 128 : 256 * x + 256] = jnp.zeros((4, 5, 5, 128), F32)
+        ry[1] = jnp.zeros((4, 40, 256), F32)
+
+    @unless(inside[(0, -1)])
+    def _():
+        for x in range(2):
+            nfy[1, :, :, :, 256 * x : 256 * x + 128] = jnp.zeros((4, 5, 5, 128), F32)
+        ry[0] = jnp.zeros((4, 40, 256), F32)
+
+    for n, (dx, dy) in enumerate(DIRS):
+
+        @unless(exists(-dx, -dy))
+        def _():
+            r2[n] = jnp.zeros((128, 128), F32)
+            r3[n] = jnp.zeros((128, 128), F32)
+
+    pl.semaphore_wait(barrier, greeted)
 
     sent = []
 
-    def send(src, dst, ssem, rsem, to):
+    def send(src, dst, ssem, rsem, dx, dy):
         copy = pltpu.make_async_remote_copy(
-            src_ref=src, dst_ref=dst, send_sem=ssem, recv_sem=rsem, device_id=to, device_id_type=MESH
+            src_ref=src, dst_ref=dst, send_sem=ssem, recv_sem=rsem, device_id=peer(dx, dy), device_id_type=MESH
         )
-        copy.start()
-        sent.append(copy)
-        return copy
+
+        @pl.when(exists(dx, dy))
+        def _():
+            copy.start()
+
+        sent.append((copy, dx, dy))
+        return sent[-1]
+
+    def receive(copies):
+        for copy, dx, dy in copies:
+
+            @pl.when(exists(-dx, -dy))
+            def _():
+                copy.wait_recv()
 
     first = [
-        send(xx.at[:, 4, :, 1, 0, :], nfx.at[1, :, :, pl.ds(0, 256)], ssem1.at[0], rsem1.at[0], peer(1, 0)),
-        send(xx.at[:, 0, :, 0, 0, :], nfx.at[0, :, :, pl.ds(256, 256)], ssem1.at[1], rsem1.at[1], peer(-1, 0)),
+        send(xx.at[:, 4, :, 1, 0, :], nfx.at[1, :, :, pl.ds(0, 256)], ssem1.at[0], rsem1.at[0], 1, 0),
+        send(xx.at[:, 0, :, 0, 0, :], nfx.at[0, :, :, pl.ds(256, 256)], ssem1.at[1], rsem1.at[1], -1, 0),
     ]
     for x in range(2):
         first.append(
             send(xy.at[:, :, 4, :, x, 1, 0, :], nfy.at[1, :, :, :, pl.ds(256 * x, 128)],
-                 ssem1.at[2 + 2 * x], rsem1.at[2 + 2 * x], peer(0, 1))
+                 ssem1.at[2 + 2 * x], rsem1.at[2 + 2 * x], 0, 1)
         )
         first.append(
             send(xy.at[:, :, 0, :, x, 0, 0, :], nfy.at[0, :, :, :, pl.ds(256 * x + 128, 128)],
-                 ssem1.at[3 + 2 * x], rsem1.at[3 + 2 * x], peer(0, -1))
+                 ssem1.at[3 + 2 * x], rsem1.at[3 + 2 * x], 0, -1)
         )
 
     for copy in local[0:4]:
@@ -282,30 +338,17 @@
     for piece, target in zip(split(pinv[...]), (mi_h, mi_l)):
         target[...] = dot_nt(dot(order, piece).astype(BF16), order).astype(BF16)
 
-    has = {
-        (1, 0): jnp.where(px < nx - 1, 1.0, 0.0),
-        (-1, 0): jnp.where(px > 0, 1.0, 0.0),
-        (0, 1): jnp.where(py < ny - 1, 1.0, 0.0),
-        (0, -1): jnp.where(py > 0, 1.0, 0.0),
-    }
-    lane = iota((1, LANES), 1)
-    upper_x = jnp.where(lane >= 256, has[(1, 0)], 1.0)
-    lower_x = jnp.where(lane < 256, has[(-1, 0)], 1.0)
-    upper_y = jnp.where(((lane >> 7) & 1) == 1, has[(0, 1)], 1.0)
-    lower_y = jnp.where(((lane >> 7) & 1) == 0, has[(0, -1)], 1.0)
-
     for copy in local[9:]:
         copy.wait()
-    for copy in first:
-        copy.wait_recv()
+    receive(first)
 
     for f in range(4):
         parts = [
-            rows_to(nfx[0, f], 32) * upper_x,
-            rows_to(nfx[1, f], 32) * lower_x,
+            rows_to(nfx[0, f], 32),
+            rows_to(nfx[1, f], 32),
         ]
-        parts += [rows_to(nfy[0, f, i], 8) * upper_y for i in range(5)]
-        parts += [rows_to(nfy[1, f, i], 8) * lower_y for i in range(5)]
+        parts += [rows_to(nfy[0, f, i], 8) for i in range(5)]
+        parts += [rows_to(nfy[1, f, i], 8) for i in range(5)]
         parts.append(by_column(from_next, rows_to(nfz[0, f], 32)))
         parts.append(by_column(from_previous, rows_to(nfz[1, f], 32)))
         parts.append(jnp.zeros((48, LANES), F32))
@@ -351,7 +394,7 @@
                 sbuf[n, pl.ds(at, v.shape[0]), :] = v
                 at += v.shape[0]
             copies.append(
-                send(sbuf.at[n, pl.ds(0, at)], rbuf.at[n, pl.ds(0, at)], ssem.at[n], rsem.at[n], peer(dx, dy))
+                send(sbuf.at[n, pl.ds(0, at)], rbuf.at[n, pl.ds(0, at)], ssem.at[n], rsem.at[n], dx, dy)
             )
         return copies
 
@@ -381,22 +424,13 @@
             sy[0, f, :, pl.ds(128 * x, 128)] = fz[f, 64:104, 256 * x + 128 : 256 * x + 256]
             sy[1, f, :, pl.ds(128 * x, 128)] = fz[f, 104:144, 256 * x : 256 * x + 128]
     whole = [
-        send(sx.at[0], rx.at[0], ssemf.at[0], rsemf.at[0], peer(1, 0)),
-        send(sx.at[1], rx.at[1], ssemf.at[1], rsemf.at[1], peer(-1, 0)),
-        send(sy.at[0], ry.at[0], ssemf.at[2], rsemf.at[2], peer(0, 1)),
-        send(sy.at[1], ry.at[1], ssemf.at[3], rsemf.at[3], peer(0, -1)),
+        send(sx.at[0], rx.at[0], ssemf.at[0], rsemf.at[0], 1, 0),
+        send(sx.at[1], rx.at[1], ssemf.at[1], rsemf.at[1], -1, 0),
+        send(sy.at[0], ry.at[0], ssemf.at[2], rsemf.at[2], 0, 1),
+        send(sy.at[1], ry.at[1], ssemf.at[3], rsemf.at[3], 0, -1),
     ]
 
-    def sender_is_there(dx, dy):
-        there = 1.0
-        if dx:
-            there = there * has[(-dx, 0)]
-        if dy:
-            there = there * has[(0, -dy)]
-        return there
-
-    for copy in second:
-        copy.wait_recv()
+    receive(second)
     field_of = {}
 
     def put(at, v):
@@ -410,24 +444,23 @@
         late += [("b", 0, (y, 2), hy[(1, y)]), ("b", 1, (y, -1), hy[(-1, y)])]
     for n, (dx, dy) in enumerate(DIRS):
         x, y = edge(dx), edge(dy)
-        there = sender_is_there(dx, dy)
         side_a, side_b = (0 if dx == 1 else 1), (0 if dy == 1 else 1)
         if dy == 0:
             for t in range(2):
                 put((x - 2 * dx, t), r2[n, 32 * t : 32 * t + 32, :])
-                late.append(("a", side_a, (x - dx, t), r2[n, 64 + 16 * t : 80 + 16 * t, :] * there))
-            late.append(("b", 0, (x - 2 * dx, 2), r2[n, 96:112, :] * there))
-            late.append(("b", 1, (x - 2 * dx, -1), r2[n, 112:128, :] * there))
+                late.append(("a", side_a, (x - dx, t), r2[n, 64 + 16 * t : 80 + 16 * t, :]))
+            late.append(("b", 0, (x - 2 * dx, 2), r2[n, 96:112, :]))
+            late.append(("b", 1, (x - 2 * dx, -1), r2[n, 112:128, :]))
         elif dx == 0:
             for t in range(2):
                 put((t, y - 2 * dy), r2[n, 32 * t : 32 * t + 32, :])
-                late.append(("b", side_b, (t, y - dy), r2[n, 64 + 16 * t : 80 + 16 * t, :] * there))
-            late.append(("a", 0, (2, y - 2 * dy), r2[n, 96:112, :] * there))
-            late.append(("a", 1, (-1, y - 2 * dy), r2[n, 112:128, :] * there))
+                late.append(("b", side_b, (t, y - dy), r2[n, 64 + 16 * t : 80 + 16 * t, :]))
+            late.append(("a", 0, (2, y - 2 * dy), r2[n, 96:112, :]))
+            late.append(("a", 1, (-1, y - 2 * dy), r2[n, 112:128, :]))
         else:
             put((x - 2 * dx, y - 2 * dy), r2[n, 0:32, :])
-            late.append(("a", side_a, (x - dx, y - 2 * dy), r2[n, 32:48, :] * there))
-            late.append(("b", side_b, (x - 2 * dx, y - dy), r2[n, 48:64, :] * there))
+            late.append(("a", side_a, (x - dx, y - 2 * dy), r2[n, 32:48, :]))
+            late.append(("b", side_b, (x - 2 * dx, y - dy), r2[n, 48:64, :]))
     for kind, side, at, v in late:
         field_of[at] = add_a(field_of[at], side, v) if kind == "a" else add_b(field_of[at], side, v)
 
@@ -486,19 +519,18 @@
 
     third = exchange(correction_blocks, s3, r3, ssem3, rsem3)
 
-    for copy in whole:
-        copy.wait_recv()
+    receive(whole)
     for f in range(4):
-        x_up = jnp.concatenate([fz[f, 32:64, 256:512], rx[1, f]], axis=1) * upper_x
-        x_down = jnp.concatenate([rx[0, f], fz[f, 0:32, 0:256]], axis=1) * lower_x
+        x_up = jnp.concatenate([fz[f, 32:64, 256:512], rx[1, f]], axis=1)
+        x_down = jnp.concatenate([rx[0, f], fz[f, 0:32, 0:256]], axis=1)
         y_up, y_down = [], []
         for x in range(2):
             y_up += [fz[f, 104:144, 256 * x + 128 : 256 * x + 256], ry[1, f, :, 128 * x : 128 * x + 128]]
             y_down += [ry[0, f, :, 128 * x : 128 * x + 128], fz[f, 64:104, 256 * x : 256 * x + 128]]
         parts = [
             x_up, x_down,
-            jnp.concatenate(y_up, axis=1) * upper_y,
-            jnp.concatenate(y_down, axis=1) * lower_y,
+            jnp.concatenate(y_up, axis=1),
+            jnp.concatenate(y_down, axis=1),
             by_column(from_next, fz[f, 176:208, :]),
             by_column(from_previous, fz[f, 144:176, :]),
             jnp.zeros((48, LANES), F32),
@@ -506,8 +538,7 @@
         around = mm3(bte_h[...], bte_l[...], jnp.concatenate(parts, axis=0))
         xhat[f] = 0.2 * xhat[f] + 0.8 * (dinv[...] * (bhat[f] + 0.5 * around))
 
-    for copy in third:
-        copy.wait_recv()
+    receive(third)
     fixed = {at: spread[at] for at in own}
     near_x = {(2, y): a_half(spread[(2, y)], 0) for y in range(2)} | {
         (-1, y): a_half(spread[(-1, y)], 1) for y in range(2)
@@ -542,10 +573,10 @@
             rims.append(
                 jnp.concatenate(
                     [
-                        a_half(fixed[(1, y)], 0) if x == 0 else near_x[(2, y)] * has[(1, 0)],
-                        a_half(fixed[(0, y)], 1) if x == 1 else near_x[(-1, y)] * has[(-1, 0)],
-                        b_half(fixed[(x, 1)], 0) if y == 0 else near_y[(x, 2)] * has[(0, 1)],
-                        b_half(fixed[(x, 0)], 1) if y == 1 else near_y[(x, -1)] * has[(0, -1)],
+                        a_half(fixed[(1, y)], 0) if x == 0 else near_x[(2, y)],
+                        a_half(fixed[(0, y)], 1) if x == 1 else near_x[(-1, y)],
+                        b_half(fixed[(x, 1)], 0) if y == 0 else near_y[(x, 2)],
+                        b_half(fixed[(x, 0)], 1) if y == 1 else near_y[(x, -1)],
                         jnp.where(up_row, from_previous(v), from_next(v)),
                         jnp.zeros((32, 128), F32),
                     ],
@@ -563,8 +594,11 @@
         value = mm3(bb_h[...], bb_l[...], final)
         for c in range(4):
             outv[pl.ds(500 * f + c, 125, stride=4), :] = value[0:125, 128 * c : 128 * c + 128]
-    for copy in sent:
-        copy.wait_send()
+    for copy, dx, dy in sent:
+
+        @pl.when(exists(dx, dy))
+        def _():
+            copy.wait_send()
 
 
 def solution(mesh):

time: 33.6 us -> 28 us (0.83)
  the two profiles are of different devices: /device:TPU:1 before, /device:TPU:37 now
where the time goes in v2:
time: 28 us; the launch traced here: 27.9 us
  Pallas kernels  26.9 us (96%)
  local copies, waits for them, and re-layouts  0.96 us (3%)
    pallas_call x1, Pallas kernels, per_device(): pl.pallas_call(body, out_shape=pltpu.VMEM((2000, 128), F32), in_specs=[hb...  26.9 us
    unnamed x1, local copies, waits for them, and re-layouts  0.96 us

profile of v2, /device:TPU:37, one launch (start us, length us, event | category | flops | bytes accessed | tf_op | source)
XLA Modules:
  0.0 27.9 jit_solution(1852065609714051616)
XLA Ops:
  0.0 26.9 %shard_map.91 = f32[2000,128]{1,0:T(8,128)S(1)} custom-call(f32[4,125,1,512]{3,2,1,0:T(1,128)} %bitcast.10, f32[4,5,25,2,1,256]{5,4,3,2,1,0:T(1,128)} %bitcast.11, f32[4,5,5,5,2,2,1,128]{7,6,5,4,3,2,1,0:T(1,128)} %bitcast.12, f32[4,25,5,1,512]{4,3,2,1,0:T(1,128)} %bitcast.13, f32[4,125,1,512]{3,2,1,0:T(1,128)} %bitcast.14, f32[4,128]{1,0:T(4,128)} %bitcast.17, ...), custom_call_target="tpu_custom_call" | custom-call | tf_op jit(solution)/shard_map/pallas_call | solution.py:626
  26.9 1.0 %copy.11 = f32[4,5,5,5,2,2,128]{6,5,4,3,2,1,0:T(2,128)} copy(f32[4,5,5,5,2,2,128]{6,5,4,3,2,1,0:T(2,128)S(1)} %bitcast.9) | data formatting | bytes 2048000

commit v3 on v2

--- a/solution.py
+++ b/solution.py
@@ -11,7 +11,7 @@
 MESH = pl.DeviceIdType.MESH
 F32 = jnp.float32
 BF16 = jnp.bfloat16
-DIRS = ((1, 0), (-1, 0), (0, 1), (0, -1), (1, 1), (1, -1), (-1, 1), (-1, -1))
+DIRS = ((1, 1), (1, -1), (-1, 1), (-1, -1), (1, 0), (-1, 0), (0, 1), (0, -1))
 LANES = 512
 
 
@@ -120,7 +120,7 @@
     outv,
     ub, mv, xin, bin_, nfx, nfy, nfz, coef, pinv, pe, pm, tab,
     bt_h, bt_l, bte_h, bte_l, bb_h, bb_l, fb_h, fb_l,
-    qc_h, qc_l, qf_h, qf_l, tc, tf_h, tf_l, mi_h, mi_l,
+    qc, qf, tc, tf_h, tf_l, mi_h, mi_l,
     xhat, bhat, dinv, oh, xs_h, xs_l, ts_h, ts_l,
     cp, gath, wh, wl, ans, ap, vv,
     sx, sy, rx, ry, fz, s2, r2, s3, r3,
@@ -167,7 +167,7 @@
 
     barrier = pltpu.get_barrier_semaphore()
     greeted = 0
-    for dx, dy in DIRS:
+    for dx, dy in DIRS[4:]:
         greeted = greeted + jnp.where(exists(dx, dy), 1, 0)
 
         @pl.when(exists(dx, dy))
@@ -271,7 +271,9 @@
 
     nodes = block(0)
     bt_h[...], bt_l[...] = split(nodes)
-    bb_h[...], bb_l[...] = split(nodes.T)
+    high, low = split(nodes.T)
+    bb_h[...] = jnp.concatenate([high, high], axis=1)
+    bb_l[...] = low
     for part in range(2):
         faces = block(128 + 128 * part)
         span = pl.ds(128 * part, 128)
@@ -284,15 +286,19 @@
         part = jnp.where(field == f, coarse_block, 0.0)
         high, low = split(part)
         tc[pl.ds(128 * f, 128), :] = jnp.where(copy_of < 64, high.astype(F32), low.astype(F32)).astype(BF16)
-        turned = part.T
-        qc_h[:, pl.ds(128 * f, 128)], qc_l[:, pl.ds(128 * f, 128)] = split(turned[0:32])
+        high, low = split(part.T[0:32])
+        qc[0:32, pl.ds(128 * f, 128)] = high
+        qc[32:64, pl.ds(128 * f, 128)] = low
     field = tab[3:4, 512:640]
     face_block = block(512)
     for f in range(4):
         part = jnp.where(field == f, face_block, 0.0)
-        tf_h[pl.ds(128 * f, 128), :], tf_l[pl.ds(128 * f, 128), :] = split(part)
-        turned = part.T
-        qf_h[:, pl.ds(128 * f, 128)], qf_l[:, pl.ds(128 * f, 128)] = split(turned[0:96])
+        high, low = split(part)
+        tf_h[pl.ds(128 * f, 128), :] = jnp.concatenate([high, high], axis=1)
+        tf_l[pl.ds(128 * f, 128), :] = low
+        high, low = split(part.T[0:96])
+        qf[0:96, pl.ds(128 * f, 128)] = high
+        qf[96:192, pl.ds(128 * f, 128)] = low
 
     modes = mode_index((128, 128))
     total = jnp.zeros((128, 128), F32)
@@ -363,8 +369,10 @@
         xs_h[rows, :], xs_l[rows, :] = split(x1)
         ts_h[rows, :], ts_l[rows, :] = split(rest)
 
-    inner = dot(qc_h[...], ts_h[...]) + dot(qc_h[...], ts_l[...]) + dot(qc_l[...], ts_h[...])
-    rim = 0.5 * (dot(qf_h[...], xs_h[...]) + dot(qf_h[...], xs_l[...]) + dot(qf_l[...], xs_h[...]))
+    both = dot(qc[...], ts_h[...])
+    inner = both[0:32] + both[32:64] + dot(qc[0:32, :], ts_l[...])
+    both = dot(qf[...], xs_h[...])
+    rim = 0.5 * (both[0:96] + both[96:192] + dot(qf[0:96, :], xs_l[...]))
     up_row = ((iota((32, 128), 0) & 1) == 1)
 
     def rim_of(start, size, c):
@@ -423,14 +431,13 @@
         for x in range(2):
             sy[0, f, :, pl.ds(128 * x, 128)] = fz[f, 64:104, 256 * x + 128 : 256 * x + 256]
             sy[1, f, :, pl.ds(128 * x, 128)] = fz[f, 104:144, 256 * x : 256 * x + 128]
+    receive(second)
     whole = [
         send(sx.at[0], rx.at[0], ssemf.at[0], rsemf.at[0], 1, 0),
         send(sx.at[1], rx.at[1], ssemf.at[1], rsemf.at[1], -1, 0),
         send(sy.at[0], ry.at[0], ssemf.at[2], rsemf.at[2], 0, 1),
         send(sy.at[1], ry.at[1], ssemf.at[3], rsemf.at[3], 0, -1),
     ]
-
-    receive(second)
     field_of = {}
 
     def put(at, v):
@@ -474,21 +481,28 @@
                     p = sx_ * 4 + sy_ * 2 + z
                     for t in range(2):
                         cp[pl.ds(256 * t + 32 * p, 32), pl.ds(128 * (3 * vx + vy), 128)] = pieces[t]
-    gath[...] = dot(cp[pl.ds(0, 256), :], oh[...]) + dot(cp[pl.ds(256, 256), :], oh[...])
-    for s in range(8):
-        slot = jnp.broadcast_to(place[s : s + 1, :], (32, LANES))
-        value = jnp.zeros((32, LANES), F32)
+    halves = [pl.ds(256 * h, 256) for h in range(2)]
+
+    def slots(h):
+        return [jnp.broadcast_to(place[t : t + 1, 256 * h : 256 * h + 256], (32, 256)) for t in range(8)]
+
+    for half in halves:
+        gath[:, half] = dot(cp[pl.ds(0, 256), :], oh[:, half]) + dot(cp[pl.ds(256, 256), :], oh[:, half])
+    for h, half in enumerate(halves):
+        for t, slot in enumerate(slots(h)):
+            value = jnp.zeros((32, 256), F32)
+            for p in range(8):
+                value = jnp.where(slot == p, gath[pl.ds(32 * p, 32), half], value)
+            rows = pl.ds(32 * t, 32)
+            wh[rows, half], wl[rows, half] = split(value)
+        ans[:, half] = dot(mi_h[...], wh[:, half]) + dot(mi_h[...], wl[:, half]) + dot(mi_l[...], wh[:, half])
+    for h, half in enumerate(halves):
+        places = slots(h)
         for p in range(8):
-            value = jnp.where(slot == p, gath[pl.ds(32 * p, 32), :], value)
-        rows = pl.ds(32 * s, 32)
-        wh[rows, :], wl[rows, :] = split(value)
-    ans[...] = dot(mi_h[...], wh[...]) + dot(mi_h[...], wl[...]) + dot(mi_l[...], wh[...])
-    for p in range(8):
-        value = jnp.zeros((32, LANES), F32)
-        for s in range(8):
-            slot = jnp.broadcast_to(place[s : s + 1, :], (32, LANES))
-            value = jnp.where(slot == p, ans[pl.ds(32 * s, 32), :], value)
-        ap[pl.ds(32 * p, 32), :], ap[pl.ds(256 + 32 * p, 32), :] = split(value)
+            value = jnp.zeros((32, 256), F32)
+            for t in range(8):
+                value = jnp.where(places[t] == p, ans[pl.ds(32 * t, 32), half], value)
+            ap[pl.ds(32 * p, 32), half], ap[pl.ds(256 + 32 * p, 32), half] = split(value)
     vv[...] = dot_nt(ap[pl.ds(0, 256), :], oh[...]) + dot_nt(ap[pl.ds(256, 256), :], oh[...])
     spread = {}
     for x in range(-1, 3):
@@ -586,12 +600,14 @@
     ch, cl = split(jnp.concatenate(columns, axis=1))
     stacked = jnp.concatenate([ch, cl, ch, jnp.zeros((32, LANES), BF16)], axis=0)
     rh, rl = split(jnp.concatenate(rims, axis=1))
+    rims_both = jnp.concatenate([rh, rl], axis=0)
     for f in range(4):
         rows = pl.ds(128 * f, 128)
         direct = dot(tc[rows, :], stacked)
-        coupled = dot(tf_h[rows, :], rh) + dot(tf_h[rows, :], rl) + dot(tf_l[rows, :], rh)
+        coupled = dot(tf_h[rows, :], rims_both) + dot(tf_l[rows, :], rh)
         final = xhat[f] + 0.2 * direct + 0.4 * (dinv[...] * coupled)
-        value = mm3(bb_h[...], bb_l[...], final)
+        high, low = split(final)
+        value = dot(bb_h[...], jnp.concatenate([high, low], axis=0)) + dot(bb_l[...], high)
         for c in range(4):
             outv[pl.ds(500 * f + c, 125, stride=4), :] = value[0:125, 128 * c : 128 * c + 128]
     for copy, dx, dy in sent:
@@ -633,10 +649,10 @@
                 f32(4, 125, 512), f32(4, 125, 512), f32(2, 4, 25, 512), f32(2, 4, 5, 5, 512), f32(2, 4, 25, 512),
                 f32(4, 128), f32(256, 256), pltpu.VMEM((8, 512), jnp.int32), pltpu.VMEM((8, 512), jnp.int32),
                 pltpu.VMEM((8, 640), jnp.int32),
-                b16(128, 128), b16(128, 128), b16(128, 256), b16(128, 256), b16(128, 128), b16(128, 128),
+                b16(128, 128), b16(128, 128), b16(128, 256), b16(128, 256), b16(128, 256), b16(128, 128),
                 b16(256, 128), b16(256, 128),
-                b16(32, 512), b16(32, 512), b16(96, 512), b16(96, 512),
-                b16(512, 128), b16(512, 128), b16(512, 128), b16(256, 256), b16(256, 256),
+                b16(64, 512), b16(192, 512),
+                b16(512, 128), b16(512, 256), b16(512, 128), b16(256, 256), b16(256, 256),
                 f32(4, 128, 512), f32(4, 128, 512), f32(128, 512), b16(1152, 512),
                 b16(512, 512), b16(512, 512), b16(512, 512), b16(512, 512),
                 b16(512, 1152), f32(256, 512), b16(256, 512), b16(256, 512), f32(256, 512), b16(512, 512),

time: 28 us -> 26.5 us (0.946)
  the two profiles are of different devices: /device:TPU:37 before, /device:TPU:98 now
where the time goes in v3:
time: 26.5 us; the launch traced here: 26.4 us
  Pallas kernels  25.4 us (96%)
  local copies, waits for them, and re-layouts  0.96 us (4%)
    pallas_call x1, Pallas kernels, per_device(): pl.pallas_call(body, out_shape=pltpu.VMEM((2000, 128), F32), in_specs=[hb...  25.4 us
    unnamed x1, local copies, waits for them, and re-layouts  0.96 us

profile of v3, /device:TPU:98, one launch (start us, length us, event | category | flops | bytes accessed | tf_op | source)
XLA Modules:
  0.0 26.4 jit_solution(1956524927296159461)
XLA Ops:
  0.0 25.4 %shard_map.91 = f32[2000,128]{1,0:T(8,128)S(1)} custom-call(f32[4,125,1,512]{3,2,1,0:T(1,128)} %bitcast.10, f32[4,5,25,2,1,256]{5,4,3,2,1,0:T(1,128)} %bitcast.11, f32[4,5,5,5,2,2,1,128]{7,6,5,4,3,2,1,0:T(1,128)} %bitcast.12, f32[4,25,5,1,512]{4,3,2,1,0:T(1,128)} %bitcast.13, f32[4,125,1,512]{3,2,1,0:T(1,128)} %bitcast.14, f32[4,128]{1,0:T(4,128)} %bitcast.17, ...), custom_call_target="tpu_custom_call" | custom-call | tf_op jit(solution)/shard_map/pallas_call | solution.py:642
  25.4 1.0 %copy.11 = f32[4,5,5,5,2,2,128]{6,5,4,3,2,1,0:T(2,128)} copy(f32[4,5,5,5,2,2,128]{6,5,4,3,2,1,0:T(2,128)S(1)} %bitcast.9) | data formatting | bytes 2048000

commit v4 on v3

--- a/solution.py
+++ b/solution.py
@@ -23,7 +23,7 @@
 
 
 def column_table():
-    table = np.full((8, 640), 7, np.int32)
+    table = np.full((8, 1152), 7, np.int32)
     table[3] = 9
 
     def put(column, i, j, k, f=9):
@@ -39,6 +39,11 @@
         put(232 + u * 8 + v, u, 0, v)
         put(272 + g, u, v, 4)
         put(304 + g, u, v, 0)
+    for c in range(4):
+        for g in range(25):
+            u, v = g // 5, g % 5
+            put(640 + 128 * c + g, 4 if c >= 2 else 0, u, v)
+            put(672 + 128 * c + u * 8 + v, u, 4 if c % 2 else 0, v)
     for r in range(32):
         a, b, f, c = r // 16, r // 8 % 2, r // 2 % 4, r % 2
         for copy in range(3):
@@ -120,7 +125,7 @@
     outv,
     ub, mv, xin, bin_, nfx, nfy, nfz, coef, pinv, pe, pm, tab,
     bt_h, bt_l, bte_h, bte_l, bb_h, bb_l, fb_h, fb_l,
-    qc, qf, tc, tf_h, tf_l, mi_h, mi_l,
+    sel_h, sel_l, zb, inn, qc, qf, tc, tf_h, tf_l, mi_h, mi_l,
     xhat, bhat, dinv, oh, xs_h, xs_l, ts_h, ts_l,
     cp, gath, wh, wl, ans, ap, vv,
     sx, sy, rx, ry, fz, s2, r2, s3, r3,
@@ -177,12 +182,12 @@
     @unless(inside[(1, 0)])
     def _():
         nfx[0, :, :, 256:512] = jnp.zeros((4, 25, 256), F32)
-        rx[1] = jnp.zeros((4, 32, 256), F32)
+        rx[1] = jnp.zeros((4, 25, 256), F32)
 
     @unless(inside[(-1, 0)])
     def _():
         nfx[1, :, :, 0:256] = jnp.zeros((4, 25, 256), F32)
-        rx[0] = jnp.zeros((4, 32, 256), F32)
+        rx[0] = jnp.zeros((4, 25, 256), F32)
 
     @unless(inside[(0, 1)])
     def _():
@@ -279,6 +284,10 @@
         span = pl.ds(128 * part, 128)
         bte_h[:, span], bte_l[:, span] = split(faces)
         fb_h[span, :], fb_l[span, :] = split(faces.T)
+    for c in range(4):
+        high, low = split(block(640 + 128 * c))
+        sel_h[c] = jnp.concatenate([high, high], axis=1)
+        sel_l[c] = low
     field = tab[3:4, 384:512]
     coarse_block = block(384)
     copy_of = iota((128, 128), 1)
@@ -346,33 +355,54 @@
 
     for copy in local[9:]:
         copy.wait()
-    receive(first)
-
+
+    none = jnp.zeros((32, 256), F32)
+    gap = jnp.zeros((8, 128), F32)
     for f in range(4):
         parts = [
-            rows_to(nfx[0, f], 32),
-            rows_to(nfx[1, f], 32),
+            jnp.concatenate([rows_to(nfx[0, f, :, 0:256], 32), none], axis=1),
+            jnp.concatenate([none, rows_to(nfx[1, f, :, 256:512], 32)], axis=1),
         ]
-        parts += [rows_to(nfy[0, f, i], 8) for i in range(5)]
-        parts += [rows_to(nfy[1, f, i], 8) for i in range(5)]
+        for i in range(5):
+            near = [rows_to(nfy[0, f, i, :, 256 * x : 256 * x + 128], 8) for x in range(2)]
+            parts.append(jnp.concatenate([near[0], gap, near[1], gap], axis=1))
+        for i in range(5):
+            near = [rows_to(nfy[1, f, i, :, 256 * x + 128 : 256 * x + 256], 8) for x in range(2)]
+            parts.append(jnp.concatenate([gap, near[0], gap, near[1]], axis=1))
         parts.append(by_column(from_next, rows_to(nfz[0, f], 32)))
         parts.append(by_column(from_previous, rows_to(nfz[1, f], 32)))
         parts.append(jnp.zeros((48, LANES), F32))
         around = mm3(bte_h[...], bte_l[...], jnp.concatenate(parts, axis=0))
-        loaded = bhat[f] + 0.5 * around
         x0 = xhat[f]
-        x1 = 0.2 * x0 + 0.8 * (dinv[...] * loaded)
+        zb[f] = 0.4 * (dinv[...] * (bhat[f] + 0.5 * around)) - 0.3 * x0
         diag = jnp.concatenate([diagonal(c) for c in range(4)], axis=1)
-        rest = bhat[f] - 0.2 * (diag * x0) - 0.8 * loaded
-        xhat[f] = x1
         rows = pl.ds(128 * f, 128)
-        xs_h[rows, :], xs_l[rows, :] = split(x1)
-        ts_h[rows, :], ts_l[rows, :] = split(rest)
-
+        ts_h[rows, :], ts_l[rows, :] = split(bhat[f] - diag * x0)
     both = dot(qc[...], ts_h[...])
-    inner = both[0:32] + both[32:64] + dot(qc[0:32, :], ts_l[...])
+    inn[...] = 0.2 * (both[0:32] + both[32:64] + dot(qc[0:32, :], ts_l[...]))
+
+    receive(first)
+
+    for c in range(4):
+        x, y = c // 2, c % 2
+        lanes = slice(128 * c, 128 * c + 128)
+        columns = []
+        for f in range(4):
+            parts = [rows_to(nfx[1 - x, f, :, lanes], 32)]
+            parts += [rows_to(nfy[1 - y, f, i, :, lanes], 8) for i in range(5)]
+            parts.append(jnp.zeros((56, 128), F32))
+            columns.append(jnp.concatenate(parts, axis=0))
+        high, low = split(jnp.concatenate(columns, axis=1))
+        around = dot(sel_h[c], jnp.concatenate([high, low], axis=0)) + dot(sel_l[c], high)
+        for f in range(4):
+            z = zb[f, :, lanes] + 0.2 * (dinv[:, lanes] * around[:, 128 * f : 128 * f + 128])
+            zb[f, :, lanes] = z
+            rows = pl.ds(128 * f, 128)
+            xs_h[rows, lanes], xs_l[rows, lanes] = split(z)
+
+    inner = inn[...]
     both = dot(qf[...], xs_h[...])
-    rim = 0.5 * (both[0:96] + both[96:192] + dot(qf[0:96, :], xs_l[...]))
+    rim = both[0:96] + both[96:192] + dot(qf[0:96, :], xs_l[...])
     up_row = ((iota((32, 128), 0) & 1) == 1)
 
     def rim_of(start, size, c):
@@ -418,6 +448,9 @@
 
     for f in range(4):
         rows = pl.ds(128 * f, 128)
+        x1 = 2.0 * zb[f] + 0.8 * xhat[f]
+        xhat[f] = x1
+        xs_h[rows, :], xs_l[rows, :] = split(x1)
         for part in range(2):
             span = pl.ds(128 * part, 128)
             faces = (
@@ -426,18 +459,19 @@
                 + dot(fb_l[span, :], xs_h[rows, :])
             )
             fz[f, span, :] = faces
-        sx[0, f] = fz[f, 0:32, 256:512]
-        sx[1, f] = fz[f, 32:64, 0:256]
+        sx[0, f] = fz[f, 0:25, 256:512]
+        sx[1, f] = fz[f, 32:57, 0:256]
         for x in range(2):
             sy[0, f, :, pl.ds(128 * x, 128)] = fz[f, 64:104, 256 * x + 128 : 256 * x + 256]
             sy[1, f, :, pl.ds(128 * x, 128)] = fz[f, 104:144, 256 * x : 256 * x + 128]
-    receive(second)
+    receive(second[6:])
     whole = [
         send(sx.at[0], rx.at[0], ssemf.at[0], rsemf.at[0], 1, 0),
         send(sx.at[1], rx.at[1], ssemf.at[1], rsemf.at[1], -1, 0),
         send(sy.at[0], ry.at[0], ssemf.at[2], rsemf.at[2], 0, 1),
         send(sy.at[1], ry.at[1], ssemf.at[3], rsemf.at[3], 0, -1),
     ]
+    receive(second[:6])
     field_of = {}
 
     def put(at, v):
@@ -535,8 +569,8 @@
 
     receive(whole)
     for f in range(4):
-        x_up = jnp.concatenate([fz[f, 32:64, 256:512], rx[1, f]], axis=1)
-        x_down = jnp.concatenate([rx[0, f], fz[f, 0:32, 0:256]], axis=1)
+        x_up = jnp.concatenate([fz[f, 32:64, 256:512], rows_to(rx[1, f], 32)], axis=1)
+        x_down = jnp.concatenate([rows_to(rx[0, f], 32), fz[f, 0:32, 0:256]], axis=1)
         y_up, y_down = [], []
         for x in range(2):
             y_up += [fz[f, 104:144, 256 * x + 128 : 256 * x + 256], ry[1, f, :, 128 * x : 128 * x + 128]]
@@ -648,16 +682,16 @@
                 pltpu.SMEM((5, 5), F32), pltpu.SMEM((5,), F32),
                 f32(4, 125, 512), f32(4, 125, 512), f32(2, 4, 25, 512), f32(2, 4, 5, 5, 512), f32(2, 4, 25, 512),
                 f32(4, 128), f32(256, 256), pltpu.VMEM((8, 512), jnp.int32), pltpu.VMEM((8, 512), jnp.int32),
-                pltpu.VMEM((8, 640), jnp.int32),
+                pltpu.VMEM((8, 1152), jnp.int32),
                 b16(128, 128), b16(128, 128), b16(128, 256), b16(128, 256), b16(128, 256), b16(128, 128),
                 b16(256, 128), b16(256, 128),
-                b16(64, 512), b16(192, 512),
+                b16(4, 128, 256), b16(4, 128, 128), f32(4, 128, 512), f32(32, 512), b16(64, 512), b16(192, 512),
                 b16(512, 128), b16(512, 256), b16(512, 128), b16(256, 256), b16(256, 256),
                 f32(4, 128, 512), f32(4, 128, 512), f32(128, 512), b16(1152, 512),
                 b16(512, 512), b16(512, 512), b16(512, 512), b16(512, 512),
                 b16(512, 1152), f32(256, 512), b16(256, 512), b16(256, 512), f32(256, 512), b16(512, 512),
                 f32(256, 1152),
-                f32(2, 4, 32, 256), f32(2, 4, 40, 256), f32(2, 4, 32, 256), f32(2, 4, 40, 256), f32(4, 256, 512),
+                f32(2, 4, 25, 256), f32(2, 4, 40, 256), f32(2, 4, 25, 256), f32(2, 4, 40, 256), f32(4, 256, 512),
                 f32(8, 128, 128), f32(8, 128, 128), f32(8, 128, 128), f32(8, 128, 128),
                 dma((20,)), dma((6,)), dma((6,)), dma((4,)), dma((4,)), dma((8,)), dma((8,)), dma((8,)), dma((8,)),
             ],

time: 26.5 us -> 25.4 us (0.958)
  Pallas kernels: 25.4 us -> 24.4 us
    pallas_call x1, Pallas kernels: 25.4 us -> 24.4 us  [per_device(): pl.pallas_call(body, out_shape=pltpu.VMEM((2000, 128), F32), in_specs=[hb...]
where the time goes in v4:
time: 25.4 us; the launch traced here: 25.3 us
  Pallas kernels  24.4 us (96%)
  local copies, waits for them, and re-layouts  0.96 us (4%)
    pallas_call x1, Pallas kernels, per_device(): pl.pallas_call(body, out_shape=pltpu.VMEM((2000, 128), F32), in_specs=[hb...  24.4 us
    unnamed x1, local copies, waits for them, and re-layouts  0.96 us

profile of v4, /device:TPU:98, one launch (start us, length us, event | category | flops | bytes accessed | tf_op | source)
XLA Modules:
  0.0 25.3 jit_solution(5205731460144045142)
XLA Ops:
  0.0 24.4 %shard_map.91 = f32[2000,128]{1,0:T(8,128)S(1)} custom-call(f32[4,125,1,512]{3,2,1,0:T(1,128)} %bitcast.10, f32[4,5,25,2,1,256]{5,4,3,2,1,0:T(1,128)} %bitcast.11, f32[4,5,5,5,2,2,1,128]{7,6,5,4,3,2,1,0:T(1,128)} %bitcast.12, f32[4,25,5,1,512]{4,3,2,1,0:T(1,128)} %bitcast.13, f32[4,125,1,512]{3,2,1,0:T(1,128)} %bitcast.14, f32[4,128]{1,0:T(4,128)} %bitcast.17, ...), custom_call_target="tpu_custom_call" | custom-call | tf_op jit(solution)/shard_map/pallas_call | solution.py:676
  24.4 1.0 %copy.11 = f32[4,5,5,5,2,2,128]{6,5,4,3,2,1,0:T(2,128)} copy(f32[4,5,5,5,2,2,128]{6,5,4,3,2,1,0:T(2,128)S(1)} %bitcast.9) | data formatting | bytes 2048000

commit v5 on v4

--- a/solution.py
+++ b/solution.py
@@ -127,7 +127,7 @@
     bt_h, bt_l, bte_h, bte_l, bb_h, bb_l, fb_h, fb_l,
     sel_h, sel_l, zb, inn, qc, qf, tc, tf_h, tf_l, mi_h, mi_l,
     xhat, bhat, dinv, oh, xs_h, xs_l, ts_h, ts_l,
-    cp, gath, wh, wl, ans, ap, vv,
+    cz, zz, gz, wf, ans, ap, vv,
     sx, sy, rx, ry, fz, s2, r2, s3, r3,
     lsem, ssem1, rsem1, ssemf, rsemf, ssem2, rsem2, ssem3, rsem3,
 ):
@@ -145,6 +145,15 @@
 
     def unless(condition):
         return pl.when(jnp.logical_not(condition))
+
+    barrier = pltpu.get_barrier_semaphore()
+    greeted = 0
+    for dx, dy in DIRS[4:]:
+        greeted = greeted + jnp.where(exists(dx, dy), 1, 0)
+
+        @pl.when(exists(dx, dy))
+        def _():
+            pl.semaphore_signal(barrier, inc=1, device_id=peer(dx, dy), device_id_type=MESH)
 
     local = []
 
@@ -169,15 +178,6 @@
         load(xy.at[:, :, 4, :, x, 0, 0, :], nfy.at[1, :, :, :, pl.ds(256 * x + 128, 128)])
     load(xz.at[:, :, 0, 0, :], nfz.at[0])
     load(xz.at[:, :, 4, 0, :], nfz.at[1])
-
-    barrier = pltpu.get_barrier_semaphore()
-    greeted = 0
-    for dx, dy in DIRS[4:]:
-        greeted = greeted + jnp.where(exists(dx, dy), 1, 0)
-
-        @pl.when(exists(dx, dy))
-        def _():
-            pl.semaphore_signal(barrier, inc=1, device_id=peer(dx, dy), device_id_type=MESH)
 
     @unless(inside[(1, 0)])
     def _():
@@ -343,6 +343,9 @@
     place = (at_x - low_x) * 4 + (at_y - low_y) * 2 + (at_z - low_z)
     place = jnp.where(alive, place, 99)
     vertex = iota((128, LANES), 0)
+    lowest = jnp.where(vertex == low_z, 1.0, 0.0).astype(BF16)
+    zz[0:128, :] = lowest
+    zz[128:256, :] = lowest
     for v in range(9):
         oh[pl.ds(128 * v, 128), :] = jnp.where(vertex + 128 * v == key, 1.0, 0.0).astype(BF16)
 
@@ -506,37 +509,56 @@
         field_of[at] = add_a(field_of[at], side, v) if kind == "a" else add_b(field_of[at], side, v)
 
     for (x, y), v in field_of.items():
-        moved = pltpu.roll(v, 127, 1)
-        for z, value in enumerate((v, moved)):
-            pieces = split(value)
-            for sx_, sy_ in ((0, 0), (0, 1), (1, 0), (1, 1)):
-                vx, vy = x + 1 - sx_, y + 1 - sy_
-                if 0 <= vx <= 2 and 0 <= vy <= 2:
-                    p = sx_ * 4 + sy_ * 2 + z
-                    for t in range(2):
-                        cp[pl.ds(256 * t + 32 * p, 32), pl.ds(128 * (3 * vx + vy), 128)] = pieces[t]
+        for z, value in enumerate((v, pltpu.roll(v, 127, 1))):
+            rows = pl.ds(32 * (8 * (x + 1) + 2 * (y + 1) + z), 32)
+            cz[rows, 0:128], cz[rows, 128:256] = split(value)
     halves = [pl.ds(256 * h, 256) for h in range(2)]
 
+    def row_of(v, h):
+        return jnp.broadcast_to(v[:, 256 * h : 256 * h + 256], (8, 256))
+
     def slots(h):
-        return [jnp.broadcast_to(place[t : t + 1, 256 * h : 256 * h + 256], (32, 256)) for t in range(8)]
+        return [row_of(place[t : t + 1], h) for t in range(8)]
 
     for half in halves:
-        gath[:, half] = dot(cp[pl.ds(0, 256), :], oh[:, half]) + dot(cp[pl.ds(256, 256), :], oh[:, half])
-    for h, half in enumerate(halves):
-        for t, slot in enumerate(slots(h)):
-            value = jnp.zeros((32, 256), F32)
-            for p in range(8):
-                value = jnp.where(slot == p, gath[pl.ds(32 * p, 32), half], value)
-            rows = pl.ds(32 * t, 32)
-            wh[rows, half], wl[rows, half] = split(value)
-        ans[:, half] = dot(mi_h[...], wh[:, half]) + dot(mi_h[...], wl[:, half]) + dot(mi_l[...], wh[:, half])
+        gz[:, half] = dot(cz[...], zz[:, half])
     for h, half in enumerate(halves):
         places = slots(h)
-        for p in range(8):
-            value = jnp.zeros((32, 256), F32)
-            for t in range(8):
-                value = jnp.where(places[t] == p, ans[pl.ds(32 * t, 32), half], value)
-            ap[pl.ds(32 * p, 32), half], ap[pl.ds(256 + 32 * p, 32), half] = split(value)
+        in_x, in_y = row_of(low_x, h), row_of(low_y, h)
+        x_one, x_two, y_one, y_two = in_x == 1, in_x == 2, in_y == 1, in_y == 2
+        for t in range(4):
+
+            def at(x, y, z):
+                return gz[pl.ds(32 * (8 * x + 2 * y + z) + 8 * t, 8), half]
+
+            cube = []
+            for x in range(2):
+                by_y = []
+                for y in range(4):
+                    by_y.append([
+                        jnp.where(x_two, at(x + 2, y, z), jnp.where(x_one, at(x + 1, y, z), at(x, y, z)))
+                        for z in range(2)
+                    ])
+                for y in range(2):
+                    for z in range(2):
+                        cube.append(jnp.where(y_two, by_y[y + 2][z], jnp.where(y_one, by_y[y + 1][z], by_y[y][z])))
+            for slot in range(8):
+                value = jnp.zeros((8, 256), F32)
+                for p in range(8):
+                    value = jnp.where(places[slot] == p, cube[p], value)
+                wf[pl.ds(32 * slot + 8 * t, 8), half] = value
+        wh, wl = split(wf[:, half])
+        ans[:, half] = dot(mi_h[...], wh) + dot(mi_h[...], wl) + dot(mi_l[...], wh)
+    for h, half in enumerate(halves):
+        places = slots(h)
+        for t in range(4):
+            solved = [ans[pl.ds(32 * slot + 8 * t, 8), half] for slot in range(8)]
+            for p in range(8):
+                value = jnp.zeros((8, 256), F32)
+                for slot in range(8):
+                    value = jnp.where(places[slot] == p, solved[slot], value)
+                wf[pl.ds(32 * p + 8 * t, 8), half] = value
+        ap[0:256, half], ap[256:512, half] = split(wf[:, half])
     vv[...] = dot_nt(ap[pl.ds(0, 256), :], oh[...]) + dot_nt(ap[pl.ds(256, 256), :], oh[...])
     spread = {}
     for x in range(-1, 3):
@@ -689,7 +711,7 @@
                 b16(512, 128), b16(512, 256), b16(512, 128), b16(256, 256), b16(256, 256),
                 f32(4, 128, 512), f32(4, 128, 512), f32(128, 512), b16(1152, 512),
                 b16(512, 512), b16(512, 512), b16(512, 512), b16(512, 512),
-                b16(512, 1152), f32(256, 512), b16(256, 512), b16(256, 512), f32(256, 512), b16(512, 512),
+                b16(1024, 256), b16(256, 512), f32(1024, 512), f32(256, 512), f32(256, 512), b16(512, 512),
                 f32(256, 1152),
                 f32(2, 4, 25, 256), f32(2, 4, 40, 256), f32(2, 4, 25, 256), f32(2, 4, 40, 256), f32(4, 256, 512),
                 f32(8, 128, 128), f32(8, 128, 128), f32(8, 128, 128), f32(8, 128, 128),

time: 25.4 us -> 25 us (0.984)
  Pallas kernels: 24.4 us -> 24 us
    pallas_call x1, Pallas kernels: 24.4 us -> 24 us  [per_device(): pl.pallas_call(body, out_shape=pltpu.VMEM((2000, 128), F32), in_specs=[hb...]
where the time goes in v5:
time: 25 us; the launch traced here: 24.9 us
  Pallas kernels  24 us (96%)
  local copies, waits for them, and re-layouts  0.96 us (4%)
    pallas_call x1, Pallas kernels, per_device(): pl.pallas_call(body, out_shape=pltpu.VMEM((2000, 128), F32), in_specs=[hb...  24 us
    unnamed x1, local copies, waits for them, and re-layouts  0.96 us

profile of v5, /device:TPU:98, one launch (start us, length us, event | category | flops | bytes accessed | tf_op | source)
XLA Modules:
  0.0 24.9 jit_solution(2653483986579881211)
XLA Ops:
  0.0 24.0 %shard_map.91 = f32[2000,128]{1,0:T(8,128)S(1)} custom-call(f32[4,125,1,512]{3,2,1,0:T(1,128)} %bitcast.10, f32[4,5,25,2,1,256]{5,4,3,2,1,0:T(1,128)} %bitcast.11, f32[4,5,5,5,2,2,1,128]{7,6,5,4,3,2,1,0:T(1,128)} %bitcast.12, f32[4,25,5,1,512]{4,3,2,1,0:T(1,128)} %bitcast.13, f32[4,125,1,512]{3,2,1,0:T(1,128)} %bitcast.14, f32[4,128]{1,0:T(4,128)} %bitcast.17, ...), custom_call_target="tpu_custom_call" | custom-call | tf_op jit(solution)/shard_map/pallas_call | solution.py:698
  24.0 1.0 %copy.11 = f32[4,5,5,5,2,2,128]{6,5,4,3,2,1,0:T(2,128)} copy(f32[4,5,5,5,2,2,128]{6,5,4,3,2,1,0:T(2,128)S(1)} %bitcast.9) | data formatting | bytes 2048000

commit v6 on v5

--- a/solution.py
+++ b/solution.py
@@ -122,9 +122,9 @@
 def kernel(
     nx, ny,
     xa, xx, xy, xz, ba, coef_h, ub_h, mv_h, pinv_h, pe_h, pm_h, tab_h,
-    outv,
+    fin, turn,
     ub, mv, xin, bin_, nfx, nfy, nfz, coef, pinv, pe, pm, tab,
-    bt_h, bt_l, bte_h, bte_l, bb_h, bb_l, fb_h, fb_l,
+    bt_h, bt_l, bte_h, bte_l, fb_h, fb_l,
     sel_h, sel_l, zb, inn, qc, qf, tc, tf_h, tf_l, mi_h, mi_l,
     xhat, bhat, dinv, oh, xs_h, xs_l, ts_h, ts_l,
     cz, zz, gz, wf, ans, ap, vv,
@@ -277,8 +277,7 @@
     nodes = block(0)
     bt_h[...], bt_l[...] = split(nodes)
     high, low = split(nodes.T)
-    bb_h[...] = jnp.concatenate([high, high], axis=1)
-    bb_l[...] = low
+    turn[...] = jnp.concatenate([high, high, low], axis=1)
     for part in range(2):
         faces = block(128 + 128 * part)
         span = pl.ds(128 * part, 128)
@@ -662,15 +661,27 @@
         direct = dot(tc[rows, :], stacked)
         coupled = dot(tf_h[rows, :], rims_both) + dot(tf_l[rows, :], rh)
         final = xhat[f] + 0.2 * direct + 0.4 * (dinv[...] * coupled)
-        high, low = split(final)
-        value = dot(bb_h[...], jnp.concatenate([high, low], axis=0)) + dot(bb_l[...], high)
-        for c in range(4):
-            outv[pl.ds(500 * f + c, 125, stride=4), :] = value[0:125, 128 * c : 128 * c + 128]
+        fin[f, 0:128, :], fin[f, 128:256, :] = split(final)
     for copy, dx, dy in sent:
 
         @pl.when(exists(dx, dy))
         def _():
             copy.wait_send()
+
+
+def to_nodes(fin, turn, out, value, sem):
+    copies = []
+    for f in range(4):
+        pieces = fin[f]
+        nodes = dot(turn[:, 0:256], pieces) + dot(turn[:, 256:384], pieces[0:128])
+        for c in range(4):
+            value[pl.ds(500 * f + c, 125, stride=4), :] = nodes[0:125, 128 * c : 128 * c + 128]
+        start, end = 500 * f // 8 * 8, 500 * (f + 1) // 8 * 8
+        span = pl.ds(start, end - start)
+        copies.append(pltpu.make_async_copy(value.at[span], out.at[span], sem.at[f]))
+        copies[-1].start()
+    for copy in copies:
+        copy.wait()
 
 
 def solution(mesh):
@@ -695,17 +706,17 @@
             return pltpu.with_memory_space_constraint(array, pltpu.HBM)
 
         dma = pltpu.SemaphoreType.DMA
-        out = pl.pallas_call(
+        fin, turn = pl.pallas_call(
             body,
-            out_shape=pltpu.VMEM((2000, 128), F32),
+            out_shape=(pltpu.VMEM((4, 256, 512), BF16), pltpu.VMEM((128, 384), BF16)),
             in_specs=[hbm] * 12,
-            out_specs=pl.BlockSpec(memory_space=pltpu.VMEM),
+            out_specs=(pl.BlockSpec(memory_space=pltpu.VMEM),) * 2,
             scratch_shapes=[
                 pltpu.SMEM((5, 5), F32), pltpu.SMEM((5,), F32),
                 f32(4, 125, 512), f32(4, 125, 512), f32(2, 4, 25, 512), f32(2, 4, 5, 5, 512), f32(2, 4, 25, 512),
                 f32(4, 128), f32(256, 256), pltpu.VMEM((8, 512), jnp.int32), pltpu.VMEM((8, 512), jnp.int32),
                 pltpu.VMEM((8, 1152), jnp.int32),
-                b16(128, 128), b16(128, 128), b16(128, 256), b16(128, 256), b16(128, 256), b16(128, 128),
+                b16(128, 128), b16(128, 128), b16(128, 256), b16(128, 256),
                 b16(256, 128), b16(256, 128),
                 b16(4, 128, 256), b16(4, 128, 128), f32(4, 128, 512), f32(32, 512), b16(64, 512), b16(192, 512),
                 b16(512, 128), b16(512, 256), b16(512, 128), b16(256, 256), b16(256, 256),
@@ -734,6 +745,14 @@
             in_hbm(patch_mask.T),
             in_hbm(jnp.asarray(table)),
         )
+        out = pl.pallas_call(
+            to_nodes,
+            out_shape=jax.ShapeDtypeStruct((2000, 128), F32),
+            in_specs=[pl.BlockSpec(memory_space=pltpu.VMEM)] * 2,
+            out_specs=pl.BlockSpec(memory_space=pl.ANY),
+            scratch_shapes=[f32(2000, 128), dma((4,))],
+            compiler_params=pltpu.CompilerParams(vmem_limit_bytes=16 * 1024 * 1024),
+        )(fin, turn)
         return out.reshape(4, 5, 5, 5, 2, 2, 128)
 
     grid = P(None, None, None, None, "px", "py", None)

time: 25 us -> 24.5 us (0.980)
  local copies, waits for them, and re-layouts: 0.96 us -> 0 us
  Pallas kernels: 24 us -> 24.3 us
    unnamed x1 -> x0, local copies, waits for them, and re-layouts: 0.96 us -> none
    pallas_call x1 -> x2, Pallas kernels: 24 us -> 24.3 us  [the longest x1 23.1 us: per_device(): pl.pallas_call(body, out_shape=(pltpu.VMEM((4, 256, 512), BF16), pltpu.VM...]
where the time goes in v6:
time: 24.5 us; the launch traced here: 24.4 us
  Pallas kernels  24.3 us (99%)
    pallas_call x1, Pallas kernels, per_device(): pl.pallas_call(body, out_shape=(pltpu.VMEM((4, 256, 512), BF16), pltpu.VM...  23.1 us
    pallas_call x1, Pallas kernels, per_device(): pl.pallas_call(to_nodes, out_shape=jax.ShapeDtypeStruct((2000, 128), F32)...  1.2 us

profile of v6, /device:TPU:98, one launch (start us, length us, event | category | flops | bytes accessed | tf_op | source)
XLA Modules:
  0.0 24.4 jit_solution(4075562489919049183)
XLA Ops:
  0.0 23.1 %shard_map.91 = (bf16[4,256,512]{2,1,0:T(8,128)(2,1)S(1)}, bf16[128,384]{1,0:T(8,128)(2,1)S(1)}) custom-call(f32[4,125,1,512]{3,2,1,0:T(1,128)} %bitcast.9, f32[4,5,25,2,1,256]{5,4,3,2,1,0:T(1,128)} %bitcast.10, f32[4,5,5,5,2,2,1,128]{7,6,5,4,3,2,1,0:T(1,128)} %bitcast.11, f32[4,25,5,1,512]{4,3,2,1,0:T(1,128)} %bitcast.12, f32[4,125,1,512]{3,2,1,0:T(1,128)} %bitcast.13, ...), custom_call_target="tpu_custom_call" | custom-call | tf_op jit(solution)/shard_map/pallas_call | solution.py:709
  23.2 1.2 %shard_map.92 = f32[2000,128]{1,0:T(8,128)} custom-call(bf16[4,256,512]{2,1,0:T(8,128)(2,1)S(1)} %get-tuple-element.7.fin, bf16[128,384]{1,0:T(8,128)(2,1)S(1)} %get-tuple-element.8.turn), custom_call_target="tpu_custom_call" | custom-call | tf_op jit(solution)/shard_map/pallas_call | solution.py:748

commit v7 on v6

--- a/solution.py
+++ b/solution.py
@@ -750,7 +750,7 @@
             out_shape=jax.ShapeDtypeStruct((2000, 128), F32),
             in_specs=[pl.BlockSpec(memory_space=pltpu.VMEM)] * 2,
             out_specs=pl.BlockSpec(memory_space=pl.ANY),
-            scratch_shapes=[f32(2000, 128), dma((4,))],
+            scratch_shapes=[f32(2016, 128), dma((4,))],
             compiler_params=pltpu.CompilerParams(vmem_limit_bytes=16 * 1024 * 1024),
         )(fin, turn)
         return out.reshape(4, 5, 5, 5, 2, 2, 128)

time: 24.5 us -> 24.5 us (level)
  no operation moved by 1% of the time
where the time goes in v7:
time: 24.5 us; the launch traced here: 24.4 us
  Pallas kernels  24.3 us (99%)
    pallas_call x1, Pallas kernels, per_device(): pl.pallas_call(body, out_shape=(pltpu.VMEM((4, 256, 512), BF16), pltpu.VM...  23.1 us
    pallas_call x1, Pallas kernels, per_device(): pl.pallas_call(to_nodes, out_shape=jax.ShapeDtypeStruct((2000, 128), F32)...  1.2 us

profile of v7, /device:TPU:98, one launch (start us, length us, event | category | flops | bytes accessed | tf_op | source)
XLA Modules:
  0.0 24.4 jit_solution(4075562489919049183)
XLA Ops:
  0.0 23.1 %shard_map.91 = (bf16[4,256,512]{2,1,0:T(8,128)(2,1)S(1)}, bf16[128,384]{1,0:T(8,128)(2,1)S(1)}) custom-call(f32[4,125,1,512]{3,2,1,0:T(1,128)} %bitcast.9, f32[4,5,25,2,1,256]{5,4,3,2,1,0:T(1,128)} %bitcast.10, f32[4,5,5,5,2,2,1,128]{7,6,5,4,3,2,1,0:T(1,128)} %bitcast.11, f32[4,25,5,1,512]{4,3,2,1,0:T(1,128)} %bitcast.12, f32[4,125,1,512]{3,2,1,0:T(1,128)} %bitcast.13, ...), custom_call_target="tpu_custom_call" | custom-call | tf_op jit(solution)/shard_map/pallas_call | solution.py:709
  23.2 1.2 %shard_map.92 = f32[2000,128]{1,0:T(8,128)} custom-call(bf16[4,256,512]{2,1,0:T(8,128)(2,1)S(1)} %get-tuple-element.7.fin, bf16[128,384]{1,0:T(8,128)(2,1)S(1)} %get-tuple-element.8.turn), custom_call_target="tpu_custom_call" | custom-call | tf_op jit(solution)/shard_map/pallas_call | solution.py:748

commit v8 on v7

--- a/solution.py
+++ b/solution.py
@@ -466,12 +466,14 @@
         for x in range(2):
             sy[0, f, :, pl.ds(128 * x, 128)] = fz[f, 64:104, 256 * x + 128 : 256 * x + 256]
             sy[1, f, :, pl.ds(128 * x, 128)] = fz[f, 104:144, 256 * x : 256 * x + 128]
+    whole = [
+        send(sy.at[0], ry.at[0], ssemf.at[2], rsemf.at[2], 0, 1),
+        send(sy.at[1], ry.at[1], ssemf.at[3], rsemf.at[3], 0, -1),
+    ]
     receive(second[6:])
-    whole = [
+    whole += [
         send(sx.at[0], rx.at[0], ssemf.at[0], rsemf.at[0], 1, 0),
         send(sx.at[1], rx.at[1], ssemf.at[1], rsemf.at[1], -1, 0),
-        send(sy.at[0], ry.at[0], ssemf.at[2], rsemf.at[2], 0, 1),
-        send(sy.at[1], ry.at[1], ssemf.at[3], rsemf.at[3], 0, -1),
     ]
     receive(second[:6])
     field_of = {}

time: 24.5 us -> 24.5 us (level)
  no operation moved by 1% of the time
where the time goes in v8:
time: 24.5 us; the launch traced here: 24.4 us
  Pallas kernels  24.3 us (99%)
    pallas_call x1, Pallas kernels, per_device(): pl.pallas_call(body, out_shape=(pltpu.VMEM((4, 256, 512), BF16), pltpu.VM...  23.1 us
    pallas_call x1, Pallas kernels, per_device(): pl.pallas_call(to_nodes, out_shape=jax.ShapeDtypeStruct((2000, 128), F32)...  1.2 us

profile of v8, /device:TPU:98, one launch (start us, length us, event | category | flops | bytes accessed | tf_op | source)
XLA Modules:
  0.0 24.4 jit_solution(11614536463155473026)
XLA Ops:
  0.0 23.1 %shard_map.91 = (bf16[4,256,512]{2,1,0:T(8,128)(2,1)S(1)}, bf16[128,384]{1,0:T(8,128)(2,1)S(1)}) custom-call(f32[4,125,1,512]{3,2,1,0:T(1,128)} %bitcast.9, f32[4,5,25,2,1,256]{5,4,3,2,1,0:T(1,128)} %bitcast.10, f32[4,5,5,5,2,2,1,128]{7,6,5,4,3,2,1,0:T(1,128)} %bitcast.11, f32[4,25,5,1,512]{4,3,2,1,0:T(1,128)} %bitcast.12, f32[4,125,1,512]{3,2,1,0:T(1,128)} %bitcast.13, ...), custom_call_target="tpu_custom_call" | custom-call | tf_op jit(solution)/shard_map/pallas_call | solution.py:711
  23.2 1.2 %shard_map.92 = f32[2000,128]{1,0:T(8,128)} custom-call(bf16[4,256,512]{2,1,0:T(8,128)(2,1)S(1)} %get-tuple-element.7.fin, bf16[128,384]{1,0:T(8,128)(2,1)S(1)} %get-tuple-element.8.turn), custom_call_target="tpu_custom_call" | custom-call | tf_op jit(solution)/shard_map/pallas_call | solution.py:750
